TPU v7x, 32 devices: a whole 2x2x4 slice. The times are simulated.
32 devices in a mesh: parts: 2 (over x), ctx: 16 (over z, y, core).
Axes of the slice: x: 2, y: 2, z: 4, core: 2. Of those that a mesh axis runs over, the one named last changes fastest.
Arguments:
- values: bfloat16 [4096, 2048], P(('parts', 'ctx')), parts along dimension 0, may hold values from -6 to 6
- gating: bfloat16 [4096, 2048], P(('parts', 'ctx')), parts along dimension 0, may hold values from -6 to 6
- out_weight: bfloat16 [4096, 2048], P(('parts', 'ctx')), parts along dimension 0, may hold values from -0.125 to 0.125
- residue: float32 [4096, 64], P('parts'), parts along dimension 0, may hold values from -0.03125 to 0.03125
- decay_rate: float32 [32, 64], P('parts'), parts along dimension 0, may hold values from 0.2 to 400
- skip_gain: float32 [4096], P('parts'), parts along dimension 0, may hold values from 0.5 to 1.5
- cotangent: bfloat16 [4096, 2048], P(('parts', 'ctx')), parts along dimension 0, may hold values from -6 to 6
Outputs:
- output: bfloat16 [4096, 2048], P(('parts', 'ctx')), parts along dimension 0
- value_grad: bfloat16 [4096, 2048], P(('parts', 'ctx')), parts along dimension 0
- gate_grad: bfloat16 [4096, 2048], P(('parts', 'ctx')), parts along dimension 0
- weight_grad: float32 [4096, 2048], P(('parts', 'ctx')), parts along dimension 0
There are 2 independent parts, one for each index of `parts`. A program takes and returns all parts, laid end to end along the dimension named above; each array names one. Nothing has to cross between parts.
All inputs are finite; a program needn't handle non-finite values.
Results may differ from a plain program's by a relative error of at most 0.0049.
Values may be sent and summed in bfloat16 or wider, within the bound.
A program may use at most 192 MiB of HBM per device.

v0:
```python
import jax
import jax.numpy as jnp
from jax import lax
from jax.sharding import PartitionSpec as P

BLOCK = 16


HIGHEST = lax.Precision.HIGHEST
SPLIT = lax.Precision.HIGH


def entering(value, axis, join, neutral, backward):
    count, mine = (lax.axis_size(axis), lax.axis_index(axis))
    pieces = jax.tree.map(lambda part: lax.all_gather(part, axis), value)
    if backward:
        pieces = jax.tree.map(lambda part: part[::-1], pieces)
        mine = count - 1 - mine
    so_far = jax.tree.map(
        lambda part, zero: jnp.full_like(part, 0) + jnp.asarray(zero, part.dtype), value, neutral
    )

    def turn(position, so_far):
        longer = join(so_far, jax.tree.map(lambda part: part[position], pieces))
        return jax.tree.map(lambda new, old: jnp.where(position < mine, new, old), longer, so_far)

    return lax.fori_loop(0, count - 1, turn, so_far)


def mode_powers(rate_table, counts, seq_total):
    return jnp.exp(-counts[:, None, None] * (rate_table[None, :, :] / seq_total))


def block_taps(residue, rate_table, seq_total):
    width, modes = residue.shape
    groups = rate_table.shape[0]
    channels = width // groups
    offsets = jnp.arange(BLOCK).astype(jnp.float32)
    res_groups = residue.reshape(groups, channels, modes)
    lag_pow = mode_powers(rate_table, offsets, seq_total)
    taps = jnp.einsum("kgn,gjn->kgj", lag_pow, res_groups, precision=HIGHEST)
    return taps.reshape(BLOCK, width)


def block_parts(signal, taps, rate_table, seq_total):
    tokens, width = signal.shape
    groups, modes = rate_table.shape
    channels = width // groups
    blocks = tokens // BLOCK
    offsets = jnp.arange(BLOCK).astype(jnp.float32)
    pieces = signal.reshape(blocks, BLOCK, width)
    inner_part = taps[0][None, None, :] * pieces
    for lag in range(1, BLOCK):
        shifted = jnp.pad(pieces[:, : BLOCK - lag, :], ((0, 0), (lag, 0), (0, 0)))
        inner_part = inner_part + taps[lag][None, None, :] * shifted
    tail_pow = mode_powers(rate_table, BLOCK - 1.0 - offsets, seq_total)
    grouped = pieces.reshape(blocks, BLOCK, groups, channels)
    local_end = jnp.einsum("sgn,bsgj->bgnj", tail_pow, grouped, precision=SPLIT)
    block_index = jnp.arange(blocks).astype(jnp.float32)
    whole_pow = mode_powers(rate_table, BLOCK * (blocks - 1.0 - block_index), seq_total)
    device_end = jnp.einsum("bgn,bgnj->gnj", whole_pow, local_end, precision=SPLIT)
    device_decay = mode_powers(rate_table, jnp.full((1,), float(tokens), jnp.float32), seq_total)[
        0
    ][:, :, None]
    return (inner_part, local_end, device_end, device_decay)


def finish_conv(signal, inner_part, local_end, incoming, residue, rate_table, skip_gain, seq_total):
    tokens, width = signal.shape
    groups, modes = rate_table.shape
    channels = width // groups
    blocks = tokens // BLOCK
    offsets = jnp.arange(BLOCK).astype(jnp.float32)
    block_index = jnp.arange(blocks).astype(jnp.float32)
    gap_steps = block_index[:, None] - 1.0 - block_index[None, :]
    carry_pow = jnp.exp(
        -(BLOCK * jnp.maximum(gap_steps, 0.0))[:, :, None, None]
        * (rate_table / seq_total)[None, None]
    )
    carry_pow = jnp.where((gap_steps >= 0.0)[:, :, None, None], carry_pow, 0.0)
    start_state = jnp.einsum("bcgn,cgnj->bgnj", carry_pow, local_end, precision=SPLIT)
    start_state = (
        start_state
        + mode_powers(rate_table, BLOCK * block_index, seq_total)[:, :, :, None] * incoming[None]
    )
    lead_pow = mode_powers(rate_table, offsets + 1.0, seq_total)
    weighted = start_state * residue.reshape(groups, channels, modes).transpose(0, 2, 1)[None]
    cross_part = jnp.einsum("tgn,bgnj->btgj", lead_pow, weighted, precision=SPLIT).reshape(
        tokens, width
    )
    return inner_part.reshape(tokens, width) + cross_part + skip_gain[None, :] * signal


def chain_combine(earlier, later):
    return (earlier[0] * later[0], later[0] * earlier[1] + later[1])


def per_device(values, gating, out_weight, residue, decay_rate, skip_gain, cotangent):
    tokens, width = values.shape
    groups, modes = decay_rate.shape
    channels = width // groups
    seq_total = float(tokens * lax.axis_size("ctx"))
    identity = (
        jnp.ones((groups, modes, 1), jnp.float32),
        jnp.zeros((groups, modes, channels), jnp.float32),
    )
    signal = values.astype(jnp.float32)
    gate_float = gating.astype(jnp.float32)
    taps = block_taps(residue, decay_rate, seq_total)
    full_weight = lax.all_gather(out_weight, "ctx", axis=0, tiled=True)
    mixed_grad = lax.dot_general(
        cotangent, full_weight, (((1,), (1,)), ((), ())), preferred_element_type=jnp.float32
    )
    signal_back = (mixed_grad * gate_float)[::-1]
    parts_fwd = block_parts(signal, taps, decay_rate, seq_total)
    carried_fwd = entering((parts_fwd[3], parts_fwd[2]), "ctx", chain_combine, identity, False)
    parts_back = block_parts(signal_back, taps, decay_rate, seq_total)
    carried_back = entering((parts_back[3], parts_back[2]), "ctx", chain_combine, identity, True)
    conv = finish_conv(
        signal,
        parts_fwd[0],
        parts_fwd[1],
        carried_fwd[1],
        residue,
        decay_rate,
        skip_gain,
        seq_total,
    )
    mixed = (gate_float * conv).astype(jnp.bfloat16)
    output = jnp.dot(mixed, full_weight, preferred_element_type=jnp.float32)
    anti = finish_conv(
        signal_back,
        parts_back[0],
        parts_back[1],
        carried_back[1],
        residue,
        decay_rate,
        skip_gain,
        seq_total,
    )
    value_grad = anti[::-1].astype(jnp.bfloat16)
    gate_grad = (mixed_grad * conv).astype(jnp.bfloat16)
    weight_grad = lax.psum_scatter(
        lax.dot_general(
            mixed, cotangent, (((0,), (0,)), ((), ())), preferred_element_type=jnp.float32
        ),
        "ctx",
        scatter_dimension=0,
        tiled=True,
    )
    return (output.astype(jnp.bfloat16), value_grad, gate_grad, weight_grad)


def solution(mesh):
    placed = (
        P(("parts", "ctx"), None),
        P(("parts", "ctx"), None),
        P(("parts", "ctx"), None),
        P("parts", None),
        P("parts", None),
        P("parts"),
        P(("parts", "ctx"), None),
    )
    return jax.shard_map(
        per_device,
        mesh=mesh,
        in_specs=placed,
        out_specs=(
            P(("parts", "ctx"), None),
            P(("parts", "ctx"), None),
            P(("parts", "ctx"), None),
            P(("parts", "ctx"), None),
        ),
        check_vma=False,
    )
```

profile of v0, /device:TPU:0, one launch (start us, length us, event | category | flops | bytes accessed | tf_op | source)
XLA Modules:
  0.0 459.1 jit_solution(12437071816780589622)
XLA Ops:
  11.6 2.0 copy-done.3
  13.6 5.6 %fusion.13 = f32[16,64,1,128]{3,2,1,0:T(1,128)} fusion(f32[8,16,64,1]{0,3,2,1:T(1,128)S(1)} %bitcast.175, f32[8,16,64,128]{3,2,0,1:T(8,128)S(1)} %convolution_bitcast_fusion.1), kind=kOutput, calls=%fused_computation.20 | convolution fusion | flops 6291456 | bytes 4751360 | tf_op jit(solution)/shard_map/bgn,bgnj->gnj/dot_general | solution.py:61
  31.5 24.1 %all-gather = f32[256,64]{1,0:T(8,128)S(1)} all-gather(f32[16,64]{1,0:T(8,128)S(1)} %get-tuple-element.272), channel_id=2, replica_groups=mesh['parts'=2,'ctx'=16] {'ctx'}, dimensions={0}, use_global_device_ids=true | all-gather | bytes 69632 | tf_op jit(solution)/shard_map/all_gather | solution.py:15
  57.4 1.6 convolution_bitcast_fusion.2
  59.3 1.9 bitcast_bitcast_fusion
  61.3 5.8 %multiply_add_fusion.1 = f32[8,16,2048]{2,1,0:T(8,128)} fusion(f32[8,1,2048]{2,1,0:T(1,128)} %slice.246, f32[8,2,2048]{2,1,0:T(2,128)} %slice.244, f32[8,3,2048]{2,1,0:T(4,128)S(1)} %slice.242, f32[8,4,2048]{2,1,0:T(4,128)} %slice.240, f32[8,5,2048]{2,1,0:T(8,128)S(1)} %slice.238, f32[8,6,2048]{2,1,0:T(8,128)S(1)} %slice.236, f32[8,7,2048]{2,1,0:T(8,128)} %slice.234, ...), kind=kLoop, calls=%fused_computation.47 | loop fusion | flops 8388608 | bytes 9568256 | tf_op jit(solution)/shard_map/add | solution.py:55
  67.1 30.6 %all-gather.9.cloned.1.call-done = f32[256,64,128]{2,1,0:T(8,128)} async-done(((f32[16,64,128]{2,1,0:T(8,128)}), f32[256,64,128]{2,1,0:T(8,128)}) %all-gather.9.cloned.1.call-update) | async-done | bytes 8388624 | tf_op jit(solution)/shard_map/all_gather | solution.py:15
  97.7 21.5 %while.28 = (s32[]{:T(128)}, f32[16,64,128]{2,1,0:T(8,128)S(1)}, s32[]{:T(128)}, f32[16,16,64,1]{2,1,3,0:T(8,128)S(1)}, f32[16,16,64,128]{3,2,1,0:T(8,128)}, /*index=5*/s32[]{:T(128)}, s32[]{:T(128)}) while((s32[]{:T(128)}, f32[16,64,128]{2,1,0:T(8,128)S(1)}, s32[]{:T(128)}, f32[16,16,64,1]{2,1,3,0:T(8,128)S(1)}, ...), condition=%wide.region_1.2_spmd.clone, body=%wide.region_0.1_spmd.clone.sunk | while | flops 524292 | bytes 1585265 | solution.py:27
  119.2 9.0 %fusion.3 = f32[8,16,64,128]{3,0,2,1:T(8,128)S(1)} fusion(f32[16,64,128]{2,1,0:T(8,128)} %bitcast_bitcast_fusion, f32[16,64,128]{2,1,0:T(8,128)S(1)} %get-tuple-element.192, f32[8,16,64]{0,2,1:T(8,128)S(1)} %copy-done.6, f32[16,64]{1,0:T(8,128)S(1)} %get-tuple-element.271, f32[8,8]{1,0:T(8,128)S(1)} %copy-done.32, pred[8,8]{1,0:T(8,128)(4,1)S(1)} %copy-done.38, ...), kind=kOutput, calls=%fused_computation.9 | convolution fusion | flops 53608448 | bytes 9474368 | tf_op jit(solution)/shard_map/bcgn,cgnj->bgnj/dot_general | solution.py:81
  131.3 41.7 %all-gather.7.cloned.1.call-done = bf16[2048,2048]{1,0:T(8,128)(2,1)} async-done(((bf16[128,2048]{1,0:T(8,128)(2,1)}), bf16[2048,2048]{1,0:T(8,128)(2,1)}) %all-gather.7.cloned.1.call-update) | async-done | bytes 8388624 | tf_op jit(solution)/shard_map/all_gather | solution.py:110
  173.0 8.2 %multiply_convert_fusion = (bf16[128,2048]{1,0:T(8,128)(2,1)}, bf16[128,2048]{1,0:T(8,128)(2,1)S(1)}, f32[128,2048]{1,0:T(8,128)}) fusion(bf16[128,2048]{1,0:T(8,128)(2,1)S(1)} %copy-done.2, f32[2048]{0:T(1024)S(1)} %copy-done.30, f32[16,8,16,128]{3,2,1,0:T(8,128)} %bitcast.177, f32[8,16,2048]{2,1,0:T(8,128)} %multiply_add_fusion.1, ...), kind=kOutput, calls=%fused_computation.45 | convolution fusion | flops 1076363264 | bytes 14163968 | tf_op jit(solution)/shard_map/dot_general | solution.py:111
  181.2 6.8 %rev.12 = f32[128,2048]{1,0:T(8,128)S(1)} reverse(f32[128,2048]{1,0:T(8,128)} %get-tuple-element.252), dimensions={0} | reverse | bytes 2097152 | tf_op jit(solution)/shard_map/rev | solution.py:114
  188.2 1.9 convolution_bitcast_fusion
  190.2 2.1 copy-done.4
  192.3 5.6 %fusion.10 = f32[16,64,1,128]{3,2,1,0:T(1,128)} fusion(f32[8,16,64,1]{0,3,2,1:T(1,128)S(1)} %bitcast.176, f32[8,16,64,128]{3,2,0,1:T(8,128)S(1)} %convolution_bitcast_fusion), kind=kOutput, calls=%fused_computation.17 | convolution fusion | flops 6291456 | bytes 4751360 | tf_op jit(solution)/shard_map/bgn,bgnj->gnj/dot_general | solution.py:61
  198.2 8.5 %fusion.62 = f32[2048,2048]{1,0:T(8,128)} fusion(bf16[128,2048]{1,0:T(8,128)(2,1)S(1)} %get-tuple-element.251, bf16[128,2048]{1,0:T(8,128)(2,1)S(1)} %copy-done), kind=kOutput, calls=%fused_computation.88 | convolution fusion | flops 1073741824 | bytes 17825792 | tf_op jit(solution)/shard_map/dot_general | solution.py:144
  207.5 3.2 multiply_add_fusion
  210.6 2.1 convolution_convert_fusion
  212.7 58.5 %all-gather.11.cloned.1.call-done = f32[256,64,128]{2,1,0:T(8,128)} async-done(((f32[16,64,128]{2,1,0:T(8,128)}), f32[256,64,128]{2,1,0:T(8,128)}) %all-gather.11.cloned.1.call-update) | async-done | bytes 8388624 | tf_op jit(solution)/shard_map/all_gather | solution.py:15
  271.2 8.4 %rev.14 = f32[16,16,64,128]{3,2,1,0:T(8,128)} reverse(f32[16,16,64,128]{3,2,1,0:T(8,128)} %bitcast.174), dimensions={0} | reverse | bytes 16777216 | tf_op jit(solution)/shard_map/rev | solution.py:17
  279.6 22.7 %while.29 = (s32[]{:T(128)}, f32[16,64,128]{2,1,0:T(8,128)S(1)}, s32[]{:T(128)}, f32[16,16,64,1]{2,1,3,0:T(8,128)S(1)}, f32[16,16,64,128]{3,2,1,0:T(8,128)}, /*index=5*/s32[]{:T(128)}, s32[]{:T(128)}) while((s32[]{:T(128)}, f32[16,64,128]{2,1,0:T(8,128)S(1)}, s32[]{:T(128)}, f32[16,16,64,1]{2,1,3,0:T(8,128)S(1)}, ...), condition=%wide.region_3.4_spmd.clone, body=%wide.region_2.3_spmd.clone.sunk | while | flops 524292 | bytes 1585265 | solution.py:27
  302.3 9.2 %fusion.2 = f32[8,16,64,128]{3,0,2,1:T(8,128)S(1)} fusion(f32[16,64,128]{2,1,0:T(8,128)S(1)} %get-tuple-element.193, f32[16,64,128]{2,1,0:T(8,128)} %bitcast_bitcast_fusion, f32[8,16,64]{0,2,1:T(8,128)} %get-tuple-element.269, f32[16,64]{1,0:T(8,128)S(1)} %get-tuple-element.271, f32[8,8]{1,0:T(8,128)S(1)} %copy-done.33, pred[8,8]{1,0:T(8,128)(4,1)S(1)} %copy-done.39, ...), kind=kOutput, calls=%fused_computation.7 | convolution fusion | flops 53608448 | bytes 9474368 | tf_op jit(solution)/shard_map/bcgn,cgnj->bgnj/dot_general | solution.py:81
  314.4 5.1 %rev.15 = bf16[128,2048]{1,0:T(8,128)(2,1)} reverse(bf16[128,2048]{1,0:T(8,128)(2,1)S(1)} %fusion.35), dimensions={0} | reverse | bytes 1048576 | tf_op jit(solution)/shard_map/rev | solution.py:141
  319.5 133.1 %reduce-scatter.2.cloned.1.call-done = f32[128,2048]{1,0:T(8,128)} async-done(((f32[2048,2048]{1,0:T(8,128)}), f32[128,2048]{1,0:T(8,128)}) %reduce-scatter.2.cloned.1.call-update) | async-done | bytes 1048592 | tf_op jit(solution)/shard_map/reduce_scatter | solution.py:143
  (196 shorter events, 68.6 us)
Async XLA Ops:
  7.2 165.9 %copy-start = (bf16[128,2048]{1,0:T(8,128)(2,1)S(1)}, bf16[128,2048]{1,0:T(8,128)(2,1)}, u32[]{:S(2)}) copy-start(bf16[128,2048]{1,0:T(8,128)(2,1)} %param.17) | copy-start | bytes 1572868
  7.2 90.5 %all-gather.9.cloned.1.call-start = ((), (), s32[]{:S(2)}) async-start(), calls=%async_computation.3 | async-start | bytes 8912896 | tf_op jit(solution)/shard_map/all_gather | solution.py:15
  7.2 12.0 %copy-start.34 = (f32[16]{0:T(128)}, f32[16]{0:T(128)S(1)}, u32[]{:S(2)}) copy-start(f32[16]{0:T(128)S(1)} %subtract_negate_fusion) | copy-start | bytes 196
  11.5 2.1 copy-start.3
  11.6 8.5 %copy-start.2 = (bf16[128,2048]{1,0:T(8,128)(2,1)S(1)}, bf16[128,2048]{1,0:T(8,128)(2,1)}, u32[]{:S(2)}) copy-start(bf16[128,2048]{1,0:T(8,128)(2,1)} %param.11) | copy-start | bytes 1572868
  19.3 153.8 %all-gather.7.cloned.1.call-start = ((), (), s32[]{:S(2)}) async-start(), calls=%async_computation.1 | async-start | bytes 8912896 | tf_op jit(solution)/shard_map/all_gather | solution.py:110
  20.0 251.2 %all-gather.11.cloned.1.call-start = ((), (), s32[]{:S(2)}) async-start(), calls=%async_computation.4 | async-start | bytes 8912896 | tf_op jit(solution)/shard_map/all_gather | solution.py:15
  59.1 2.0 copy-start.7
  67.1 52.1 %copy-start.6 = (f32[8,16,64]{0,2,1:T(8,128)S(1)}, f32[8,16,64]{0,2,1:T(8,128)}, u32[]{:S(2)}) copy-start(f32[8,16,64]{0,2,1:T(8,128)} %get-tuple-element.269) | copy-start | bytes 98308
  67.1 52.1 %copy-start.32 = (f32[8,8]{1,0:T(8,128)S(1)}, f32[8,8]{1,0:T(8,128)}, u32[]{:S(2)}) copy-start(f32[8,8]{1,0:T(8,128)} %fusion.58) | copy-start | bytes 772
  67.1 52.1 %copy-start.38 = (pred[8,8]{1,0:T(8,128)(4,1)S(1)}, pred[8,8]{1,0:T(8,128)(4,1)}, u32[]{:S(2)}) copy-start(pred[8,8]{1,0:T(8,128)(4,1)} %subtract_compare_fusion) | copy-start | bytes 196
  119.2 9.0 %copy-start.36 = (f32[16]{0:T(128)S(1)}, f32[16]{0:T(128)}, u32[]{:S(2)}) copy-start(f32[16]{0:T(128)} %add_negate_fusion) | copy-start | bytes 196
  128.2 44.9 %copy-start.5 = (bf16[128,2048]{1,0:T(8,128)(2,1)S(1)}, bf16[128,2048]{1,0:T(8,128)(2,1)}, u32[]{:S(2)}) copy-start(bf16[128,2048]{1,0:T(8,128)(2,1)} %param.12) | copy-start | bytes 1572868
  128.2 44.9 %copy-start.30 = (f32[2048]{0:T(1024)S(1)}, f32[2048]{0:T(1024)}, u32[]{:S(2)}) copy-start(f32[2048]{0:T(1024)} %param.16) | copy-start | bytes 24580
  181.2 7.0 %copy-start.35 = (f32[16]{0:T(128)S(1)}, f32[16]{0:T(128)}, u32[]{:S(2)}) copy-start(f32[16]{0:T(128)} %copy-done.34) | copy-start | bytes 196
  190.2 2.1 copy-start.4
  197.9 254.7 %reduce-scatter.2.cloned.1.call-start = ((), (), s32[]{:S(2)}) async-start(), calls=%async_computation.2 | async-start | bytes 17825792 | tf_op jit(solution)/shard_map/reduce_scatter | solution.py:143
  207.0 3.7 slice-start
  207.4 3.2 slice-start.1
  279.6 22.7 %copy-start.33 = (f32[8,8]{1,0:T(8,128)S(1)}, f32[8,8]{1,0:T(8,128)}, u32[]{:S(2)}) copy-start(f32[8,8]{1,0:T(8,128)} %fusion.58) | copy-start | bytes 772
  279.6 22.7 %copy-start.39 = (pred[8,8]{1,0:T(8,128)(4,1)S(1)}, pred[8,8]{1,0:T(8,128)(4,1)}, u32[]{:S(2)}) copy-start(pred[8,8]{1,0:T(8,128)(4,1)} %subtract_compare_fusion) | copy-start | bytes 196
  302.3 9.2 %copy-start.37 = (f32[16]{0:T(128)S(1)}, f32[16]{0:T(128)}, u32[]{:S(2)}) copy-start(f32[16]{0:T(128)} %add_negate_fusion) | copy-start | bytes 196
  311.6 2.2 copy-start.31
  311.6 141.0 %copy-start.1 = (bf16[128,2048]{1,0:T(8,128)(2,1)S(1)}, bf16[128,2048]{1,0:T(8,128)(2,1)}, u32[]{:S(2)}) copy-start(bf16[128,2048]{1,0:T(8,128)(2,1)} %param.17) | copy-start | bytes 1572868
  (22 other events, 34.1 us)
Sparse Core Ops, SparseCore 0:
  19.4 78.2 all-gather.8
  99.8 73.1 all-gather.6
  198.0 73.1 all-gather.10
  275.7 176.8 reduce-scatter.1
where the time goes:
time: 462 us; the launch traced here: 459 us
  waiting for transfers between devices  265 us (57%)
  matrix products  56.1 us (12%)
  other arithmetic  55.9 us (12%)
  local copies, waits for them, and re-layouts  42.5 us (9%)
  blocking collectives  24.1 us (5%)
  between operations  14.5 us (3%)
    reduce_scatter x1, waiting for transfers between devices, per_device(): lax.psum_scatter(lax.dot_general(mixed, cotangent, (((0,), (0,)), ((), ()...  133 us
    all_gather x2, waiting for transfers between devices, entering(): pieces = jax.tree.map(lambda part: lax.all_gather(part, axis), value)  89 us
    select_n x30, other arithmetic, turn(): jnp.where(position < mine, new, old)  42.8 us
    all_gather x1, waiting for transfers between devices, per_device(): full_weight = lax.all_gather(out_weight, 'ctx', axis=0, tiled=True)  41.7 us
    all_gather x1, blocking collectives, entering(): pieces = jax.tree.map(lambda part: lax.all_gather(part, axis), value)  24.1 us
    dot_general x2, matrix products, finish_conv(): jnp.einsum('bcgn,cgnj->bgnj', carry_pow, local_end, precision=SPLIT)  18.2 us
    slice x23, local copies, waits for them, and re-layouts, block_parts(): shifted = jnp.pad(pieces[:, :BLOCK - lag, :], ((0, 0), (lag, 0), (0, 0)))  11.7 us
    dot_general x2, matrix products, block_parts(): jnp.einsum('bgn,bgnj->gnj', whole_pow, local_end, precision=SPLIT)  11.2 us
  transfers between devices with their start and end apart: 4, of which 4 were waited for; matrix products, arithmetic and copies ran while one was open for 26% of the time, Pallas kernels for 0%

commit v1 on v0

v1 whole, which is shorter than its diff:
```python
import functools

import jax
import jax.numpy as jnp
from jax import lax
from jax.experimental import pallas as pl
from jax.experimental.pallas import tpu as pltpu
from jax.sharding import PartitionSpec as P

B = 64
F32 = jnp.float32
BF16 = jnp.bfloat16


def dot(a, b):
    return jnp.dot(a, b, preferred_element_type=F32)


def split(a):
    hi = a.astype(BF16)
    return hi, (a - hi.astype(F32)).astype(BF16)


def dot3(a, b):
    ah, al = a
    bh, bl = split(b)
    return dot(ah, bh) + dot(ah, bl) + dot(al, bh)


def iota(shape, dim):
    return lax.broadcasted_iota(jnp.int32, shape, dim).astype(F32)


def make_taps(row_ref, rest_ref, skip_ref, taps_ref, groups):
    modes = rest_ref.shape[1]
    for g in range(groups):
        lag_pow = jnp.exp(-iota((B, modes), 0) * row_ref[g])
        taps = jnp.dot(
            lag_pow, rest_ref[g], preferred_element_type=F32, precision=lax.Precision.HIGHEST
        )
        first = (lax.broadcasted_iota(jnp.int32, taps.shape, 0) == 0).astype(F32)
        taps_ref[g] = taps + first * skip_ref[g]


def local_part(get, taps_ref, col_ref, inner_ref, ends_ref, pad_ref, g, blocks, back, lanes):
    modes = col_ref.shape[1]
    offs = iota((modes, B), 1)
    powers = jnp.exp(-(offs if back else B - 1.0 - offs) * col_ref[g])
    powers = split(powers)
    zeros = jnp.zeros((8, lanes), F32)
    if back:
        pad_ref[B : B + 8, :] = zeros
    else:
        pad_ref[0:8, :] = zeros

    def body(b, carry):
        x = get(b)
        if x.dtype == BF16:
            ends_ref[g, b] = dot(powers[0], x) + dot(powers[1], x)
        else:
            ends_ref[g, b] = dot3(powers, x)
        xf = x.astype(F32)
        if back:
            pad_ref[0:B, :] = xf
        else:
            pad_ref[8 : B + 8, :] = xf
        acc = [jnp.zeros((8, lanes), F32) for _ in range(B // 8)]
        for low in range(8):
            if low == 0:
                shifted = xf
            elif back:
                shifted = pad_ref[low : B + low, :]
            else:
                shifted = pad_ref[8 - low : B + 8 - low, :]
            for high in range(B // 8):
                k = 8 * high + low
                tap = taps_ref[g, k : k + 1, :]
                for r in range(B // 8 - high):
                    if back:
                        acc[r] = acc[r] + tap * shifted[8 * (r + high) : 8 * (r + high) + 8]
                    else:
                        acc[r + high] = acc[r + high] + tap * shifted[8 * r : 8 * r + 8]
        inner_ref[pl.ds(pl.multiple_of(b * B, B), B), g * lanes : (g + 1) * lanes] = (
            jnp.concatenate(acc, axis=0)
        )
        return carry

    lax.fori_loop(0, blocks, body, 0)


def plane_end(ends_ref, col_ref, g, blocks, back):
    step = jnp.exp(-float(B) * col_ref[g])
    total = ends_ref[g, blocks - 1 if back else 0]
    for i in range(1, blocks):
        total = step * total + ends_ref[g, blocks - 1 - i if back else i]
    return total


def finish(state, put, rest_ref, row_ref, col_ref, inner_ref, ends_ref, g, blocks, back, lanes):
    modes = col_ref.shape[1]
    offs = iota((B, modes), 0)
    lead = split(jnp.exp(-(B - offs if back else offs + 1.0) * row_ref[g]))
    step = jnp.exp(-float(B) * col_ref[g])
    for i in range(blocks):
        b = blocks - 1 - i if back else i
        cross = dot3(lead, state * rest_ref[g])
        put(b, inner_ref[b * B : (b + 1) * B, g * lanes : (g + 1) * lanes] + cross)
        state = step * state + ends_ref[g, b]


def incoming(planes_ref, col_ref, g, outer, here, span, back):
    state = jnp.zeros(planes_ref.shape[2:], F32)
    step = jnp.exp(-float(span) * col_ref[g])
    for i in range(outer - 1):
        e = outer - 1 - i if back else i
        use = e > here if back else e < here
        state = jnp.where(use, step * state + planes_ref[e, g].astype(F32), state)
    return state


def first_kernel(x_ref, row_ref, col_ref, rest_ref, skip_ref,
                 inner_ref, ends_ref, end_ref, taps_ref, pad_ref):
    groups, modes, lanes = rest_ref.shape
    blocks = x_ref.shape[0] // B
    make_taps(row_ref, rest_ref, skip_ref, taps_ref, groups)
    for g in range(groups):
        get = lambda b: x_ref[pl.ds(pl.multiple_of(b * B, B), B), g * lanes : (g + 1) * lanes]
        local_part(get, taps_ref, col_ref, inner_ref, ends_ref, pad_ref, g, blocks, False, lanes)
        end_ref[g] = plane_end(ends_ref, col_ref, g, blocks, False).astype(BF16)


def second_kernel(outer, inner_size, planes_ref, inner_ref, ends_ref, gate_ref,
                  row_ref, col_ref, rest_ref, conv_ref, mixed_ref):
    groups, modes, lanes = rest_ref.shape
    tokens = inner_ref.shape[0]
    blocks = tokens // B
    here = lax.axis_index("ctx") // inner_size
    for g in range(groups):
        def put(b, value):
            rows, cols = slice(b * B, (b + 1) * B), slice(g * lanes, (g + 1) * lanes)
            conv_ref[rows, cols] = value
            mixed_ref[rows, cols] = (gate_ref[rows, cols].astype(F32) * value).astype(BF16)

        state = incoming(planes_ref, col_ref, g, outer, here, tokens, False)
        finish(state, put, rest_ref, row_ref, col_ref, inner_ref, ends_ref, g, blocks, False, lanes)


def third_kernel(grad_ref, gate_ref, conv_ref, taps_ref, col_ref,
                 inner_ref, ends_ref, end_ref, gate_grad_ref, pad_ref):
    groups, _, lanes = taps_ref.shape
    blocks = grad_ref.shape[0] // B
    for g in range(groups):
        cols = slice(g * lanes, (g + 1) * lanes)

        def get(b):
            rows = pl.ds(pl.multiple_of(b * B, B), B)
            grad = grad_ref[rows, cols]
            gate_grad_ref[rows, cols] = (grad * conv_ref[rows, cols]).astype(BF16)
            return grad * gate_ref[rows, cols].astype(F32)

        local_part(get, taps_ref, col_ref, inner_ref, ends_ref, pad_ref, g, blocks, True, lanes)
        end_ref[g] = plane_end(ends_ref, col_ref, g, blocks, True).astype(BF16)


def fourth_kernel(outer, inner_size, planes_ref, inner_ref, ends_ref,
                  row_ref, col_ref, rest_ref, value_grad_ref):
    groups, modes, lanes = rest_ref.shape
    tokens = inner_ref.shape[0]
    blocks = tokens // B
    here = lax.axis_index("ctx") // inner_size
    for g in range(groups):
        def put(b, value):
            value_grad_ref[b * B : (b + 1) * B, g * lanes : (g + 1) * lanes] = value.astype(BF16)

        state = incoming(planes_ref, col_ref, g, outer, here, tokens, True)
        finish(state, put, rest_ref, row_ref, col_ref, inner_ref, ends_ref, g, blocks, True, lanes)


def call(kernel, outs, scratch, *args):
    return pl.pallas_call(
        kernel,
        out_shape=[jax.ShapeDtypeStruct(s, d) for s, d in outs],
        in_specs=[pl.BlockSpec(memory_space=pltpu.VMEM)] * len(args),
        out_specs=[pl.BlockSpec(memory_space=pltpu.VMEM)] * len(outs),
        scratch_shapes=scratch,
        compiler_params=pltpu.CompilerParams(vmem_limit_bytes=40 * 2**20),
    )(*args)


def local_tables(residue, decay_rate, skip_gain, seq_total, outer, inner, mine):
    width, modes = residue.shape
    groups = decay_rate.shape[0]
    lanes = width // (outer * inner)
    per_group = width // groups // lanes
    pick = lambda a: lax.dynamic_index_in_dim(a, mine, 1, keepdims=False)
    rates = jnp.repeat(decay_rate / seq_total, per_group, axis=0).reshape(outer, inner, modes)
    rate = pick(rates)
    rest = pick(residue.reshape(outer, inner, lanes, modes)).transpose(0, 2, 1)
    skip = pick(skip_gain.reshape(outer, inner, lanes))
    return rate[:, None, :], rate[:, :, None], rest, skip[:, None, :]


def per_device(inner, values, gating, out_weight, residue, decay_rate, skip_gain, cotangent):
    tokens, width = values.shape
    ctx = lax.axis_size("ctx")
    outer = ctx // inner
    modes = decay_rate.shape[1]
    lanes = width // ctx
    mine = lax.axis_index("ctx") % inner
    span = tokens * inner
    chans = outer * lanes
    planes = [[z * inner + q for q in range(inner)] for z in range(outer)]
    lines = [[z * inner + q for z in range(outer)] for q in range(inner)]
    row, col, rest, skip = local_tables(
        residue, decay_rate, skip_gain, float(tokens * ctx), outer, inner, mine
    )

    def to_channels(a):
        a = a.reshape(tokens, outer, inner, lanes).transpose(2, 0, 1, 3)
        a = lax.all_to_all(a, "ctx", 0, 0, axis_index_groups=planes, tiled=True)
        return a.reshape(span, chans)

    def to_tokens(a):
        a = a.reshape(inner, tokens, outer, lanes)
        a = lax.all_to_all(a, "ctx", 0, 0, axis_index_groups=planes, tiled=True)
        return a.transpose(1, 2, 0, 3).reshape(tokens, width)

    weight = lax.all_gather(out_weight, "ctx", axis=0, tiled=True, axis_index_groups=lines)
    cot = lax.all_gather(cotangent, "ctx", axis=0, tiled=True, axis_index_groups=planes)
    x = to_channels(values)
    gate = to_channels(gating)
    blocks = span // B
    pad = pltpu.VMEM((B + 8, lanes), F32)
    state = (outer, modes, lanes)
    ends_shape = (outer, blocks, modes, lanes)
    inner_f, ends_f, end_f, taps = call(
        first_kernel,
        [((span, chans), F32), (ends_shape, F32), (state, BF16), ((outer, B, lanes), F32)],
        [pad], x, row, col, rest, skip,
    )
    planes_f = lax.all_gather(end_f, "ctx", axis_index_groups=lines)
    conv, mixed = call(
        functools.partial(second_kernel, outer, inner),
        [((span, chans), F32), ((span, chans), BF16)],
        [], planes_f, inner_f, ends_f, gate, row, col, rest,
    )
    partial = jnp.dot(mixed, weight, preferred_element_type=F32).astype(BF16)
    output = lax.psum_scatter(
        partial, "ctx", scatter_dimension=0, tiled=True, axis_index_groups=planes
    )
    weight_part = lax.dot_general(
        mixed, cot, (((0,), (0,)), ((), ())), preferred_element_type=F32
    ).astype(BF16)
    weight_grad = lax.psum_scatter(
        weight_part, "ctx", scatter_dimension=0, tiled=True, axis_index_groups=lines
    ).astype(F32)
    grad = lax.dot_general(cot, weight, (((1,), (1,)), ((), ())), preferred_element_type=F32)
    inner_b, ends_b, end_b, gate_grad = call(
        third_kernel,
        [((span, chans), F32), (ends_shape, F32), (state, BF16), ((span, chans), BF16)],
        [pad], grad, gate, conv, taps, col,
    )
    planes_b = lax.all_gather(end_b, "ctx", axis_index_groups=lines)
    (value_grad,) = call(
        functools.partial(fourth_kernel, outer, inner),
        [((span, chans), BF16)],
        [], planes_b, inner_b, ends_b, row, col, rest,
    )
    return output, to_tokens(value_grad), to_tokens(gate_grad), weight_grad


def solution(mesh):
    rows = P(("parts", "ctx"), None)
    inner = 4
    return jax.shard_map(
        functools.partial(per_device, inner),
        mesh=mesh,
        in_specs=(rows, rows, rows, P("parts", None), P("parts", None), P("parts"), rows),
        out_specs=(rows,) * 4,
        check_vma=False,
    )
```

time: 462 us -> 181 us (0.39)
  waiting for transfers between devices: 265 us -> 77.5 us
  other arithmetic: 55.9 us -> 2.14 us
  matrix products: 56.1 us -> 12 us
  local copies, waits for them, and re-layouts: 42.5 us -> 10.1 us
  Pallas kernels: 0 us -> 15.4 us
  starting transfers between devices: 0.38 us -> 15 us
  blocking collectives: 24.1 us -> 33.9 us
    reduce_scatter x1 -> x2, waiting for transfers between devices: 133 us -> 20.6 us  [the longest x1 20.6 us: per_device(): lax.psum_scatter(partial, 'ctx', scatter_dimension=0, tiled=True, axis_in...]
    all_gather x3 -> x2, waiting for transfers between devices: 131 us -> 20.7 us  [the longest x1 20.7 us: per_device(): lax.all_gather(out_weight, 'ctx', axis=0, tiled=True, axis_index_groups=l...]
    dot_general x12 -> x3, matrix products: 56.1 us -> 12 us  [the longest x1 4.27 us: per_device(): lax.dot_general(mixed, cot, (((0,), (0,)), ((), ())), preferred_element_t...]
    select_n x30 -> x0, other arithmetic: 42.8 us -> none  [turn(): jnp.where(position < mine, new, old)]
    all_to_all x0 -> x4, waiting for transfers between devices: none -> 34.8 us  [the longest x2 20 us: to_channels(): a = lax.all_to_all(a, 'ctx', 0, 0, axis_index_groups=planes, tiled=True)]
    rev x4 -> x0, local copies, waits for them, and re-layouts: 20.4 us -> none  [the longest x2 8.43 us: entering(): pieces = jax.tree.map(lambda part: part[::-1], pieces)]
    pallas_call x0 -> x4, Pallas kernels: none -> 15.4 us  [call(): pl.pallas_call(kernel, out_shape=[jax.ShapeDtypeStruct(s, d) for s, d in...]
    all_to_all x0 -> x4, starting transfers between devices: none -> 14.8 us  [the longest x2 7.85 us: to_channels(): a = lax.all_to_all(a, 'ctx', 0, 0, axis_index_groups=planes, tiled=True)]
  transfers between devices with their start and end apart: 4 -> 8, of which waited for: 4 -> 6; matrix products, arithmetic and copies ran while one was open for 26% -> 13% of each run, Pallas kernels for 0% -> 9%
where the time goes in v1:
time: 181 us; the launch traced here: 180 us
  waiting for transfers between devices  77.5 us (43%)
  blocking collectives  33.9 us (19%)
  Pallas kernels  15.4 us (9%)
  starting transfers between devices  15 us (8%)
  between operations  14 us (8%)
  matrix products  12 us (7%)
  local copies, waits for them, and re-layouts  10.1 us (6%)
  other arithmetic  2.14 us (1%)
    all_gather x1, waiting for transfers between devices, per_device(): lax.all_gather(out_weight, 'ctx', axis=0, tiled=True, axis_index_groups=l...  20.7 us
    reduce_scatter x1, waiting for transfers between devices, per_device(): lax.psum_scatter(partial, 'ctx', scatter_dimension=0, tiled=True, axis_in...  20.6 us
    all_to_all x2, waiting for transfers between devices, to_channels(): a = lax.all_to_all(a, 'ctx', 0, 0, axis_index_groups=planes, tiled=True)  20 us
    all_gather x1, blocking collectives, per_device(): planes_f = lax.all_gather(end_f, 'ctx', axis_index_groups=lines)  17.4 us
    all_gather x1, blocking collectives, per_device(): planes_b = lax.all_gather(end_b, 'ctx', axis_index_groups=lines)  16.5 us
    pallas_call x4, Pallas kernels, call(): pl.pallas_call(kernel, out_shape=[jax.ShapeDtypeStruct(s, d) for s, d in...  15.4 us
    all_to_all x2, waiting for transfers between devices, to_tokens(): a = lax.all_to_all(a, 'ctx', 0, 0, axis_index_groups=planes, tiled=True)  14.8 us
    all_to_all x2, starting transfers between devices, to_channels(): a = lax.all_to_all(a, 'ctx', 0, 0, axis_index_groups=planes, tiled=True)  7.85 us
  transfers between devices with their start and end apart: 8, of which 6 were waited for; matrix products, arithmetic and copies ran while one was open for 13% of the time, Pallas kernels for 9%

profile of v1, /device:TPU:0, one launch (start us, length us, event | category | flops | bytes accessed | tf_op | source)
XLA Modules:
  0.0 180.0 jit_solution(9237384257285968886)
XLA Ops:
  8.7 1.4 reshape.39
  10.1 1.0 copy.45
  11.1 4.4 %all-to-all-start = ((bf16[4,128,4,128]{3,2,1,0:T(4,128)(2,1)}), bf16[4,128,4,128]{3,2,1,0:T(4,128)(2,1)S(1)}, u32[]{:S(2)}, u32[]{:S(2)}) async-start(bf16[4,128,4,128]{3,2,1,0:T(4,128)(2,1)} %bitcast.34), calls=%async_computation | async-start | bytes 1048576 | tf_op jit(solution)/shard_map/all_to_all | solution.py:220
  15.8 1.0 copy.44
  16.8 10.2 %all-to-all-done = bf16[4,128,4,128]{3,2,1,0:T(4,128)(2,1)S(1)} async-done(((bf16[4,128,4,128]{3,2,1,0:T(4,128)(2,1)}), bf16[4,128,4,128]{3,2,1,0:T(4,128)(2,1)S(1)}, u32[]{:S(2)}, u32[]{:S(2)}) %all-to-all-start) | async-done | bytes 524320 | tf_op jit(solution)/shard_map/all_to_all | solution.py:220
  27.0 3.5 %all-to-all-start.1 = ((bf16[4,128,4,128]{3,2,1,0:T(4,128)(2,1)}), bf16[4,128,4,128]{3,2,1,0:T(4,128)(2,1)S(1)}, u32[]{:S(2)}, u32[]{:S(2)}) async-start(bf16[4,128,4,128]{3,2,1,0:T(4,128)(2,1)} %bitcast.33), calls=%async_computation.1 | async-start | bytes 1048576 | tf_op jit(solution)/shard_map/all_to_all | solution.py:220
  31.3 9.8 %all-to-all-done.1 = bf16[4,128,4,128]{3,2,1,0:T(4,128)(2,1)S(1)} async-done(((bf16[4,128,4,128]{3,2,1,0:T(4,128)(2,1)}), bf16[4,128,4,128]{3,2,1,0:T(4,128)(2,1)S(1)}, u32[]{:S(2)}, u32[]{:S(2)}) %all-to-all-start.1) | async-done | bytes 524320 | tf_op jit(solution)/shard_map/all_to_all | solution.py:220
  41.2 6.3 %shard_map.102 = (f32[512,512]{1,0:T(8,128)S(1)}, f32[4,8,64,128]{3,2,1,0:T(8,128)S(1)}, bf16[4,64,128]{2,1,0:T(8,128)(2,1)S(1)}, f32[4,64,128]{2,1,0:T(8,128)S(1)}) custom-call(bf16[512,512]{1,0:T(8,128)(2,1)S(1)} %bitcast.39, f32[4,1,64]{2,1,0:T(1,128)S(1)} %constant_dynamic-slice_fusion.2.row_ref, f32[4,64,1]{2,1,0:T(8,128)S(1)} %copy.27.col_ref, ...), custom_call_target="tpu_custom_call" | custom-call | tf_op jit(solution)/shard_map/pallas_call | solution.py:180
  47.5 17.4 %all-gather = bf16[16,64,128]{2,1,0:T(8,128)(2,1)S(1)} all-gather(bf16[4,64,128]{2,1,0:T(8,128)(2,1)S(1)} %get-tuple-element.14), channel_id=2, replica_groups={{0,4,8,12},{1,5,9,13},{2,6,10,14},{3,7,11,15},{16,20,24,28},{17,21,25,2..., dimensions={0}, use_global_device_ids=true | all-gather | bytes 327680 | tf_op jit(solution)/shard_map/all_gather | solution.py:241
  65.7 4.3 %convolution_convert_fusion = bf16[512,2048]{1,0:T(8,128)(2,1)} fusion(bf16[512,512]{1,0:T(8,128)(2,1)S(1)} %get-tuple-element.17, bf16[512,2048]{1,0:T(8,128)(2,1)} %all-gather.7.cloned.1.call-done), kind=kOutput, calls=%fused_computation | convolution fusion | flops 1074790400 | bytes 4718592 | tf_op jit(solution)/shard_map/dot_general | solution.py:251
  70.0 20.7 %all-gather.5.cloned.1.call-done = bf16[512,2048]{1,0:T(8,128)(2,1)} async-done(((bf16[128,2048]{1,0:T(8,128)(2,1)}), bf16[512,2048]{1,0:T(8,128)(2,1)}) %all-gather.5.cloned.1.call-update) | async-done | bytes 2097168 | tf_op jit(solution)/shard_map/all_gather | solution.py:228
  90.7 4.2 %convolution_convert_fusion.1 = bf16[512,2048]{1,0:T(8,128)(2,1)} fusion(bf16[512,512]{1,0:T(8,128)(2,1)S(1)} %get-tuple-element.17, bf16[512,2048]{1,0:T(8,128)(2,1)} %all-gather.5.cloned.1.call-done), kind=kOutput, calls=%fused_computation.1 | convolution fusion | flops 1074790400 | bytes 4718592 | tf_op jit(solution)/shard_map/dot_general | solution.py:247
  94.9 3.5 %fusion.grad_ref = f32[512,512]{1,0:T(8,128)S(1)} fusion(bf16[512,2048]{1,0:T(8,128)(2,1)} %all-gather.7.cloned.1.call-done, bf16[512,2048]{1,0:T(8,128)(2,1)} %all-gather.5.cloned.1.call-done), kind=kOutput, calls=%fused_computation.11 | convolution fusion | flops 1073741824 | bytes 5242880 | tf_op jit(solution)/shard_map/dot_general | solution.py:257
  98.4 7.7 %shard_map.104 = (f32[512,512]{1,0:T(8,128)S(1)}, f32[4,8,64,128]{3,2,1,0:T(8,128)S(1)}, bf16[4,64,128]{2,1,0:T(8,128)(2,1)S(1)}, bf16[512,512]{1,0:T(8,128)(2,1)S(1)}) custom-call(f32[512,512]{1,0:T(8,128)S(1)} %fusion.grad_ref, bf16[512,512]{1,0:T(8,128)(2,1)S(1)} %bitcast.38, f32[512,512]{1,0:T(8,128)S(1)} %get-tuple-element.18.conv_ref, ...), custom_call_target="tpu_custom_call" | custom-call | tf_op jit(solution)/shard_map/pallas_call | solution.py:180
  106.2 16.5 %all-gather.1 = bf16[16,64,128]{2,1,0:T(8,128)(2,1)S(1)} all-gather(bf16[4,64,128]{2,1,0:T(8,128)(2,1)S(1)} %get-tuple-element.20), channel_id=3, replica_groups={{0,4,8,12},{1,5,9,13},{2,6,10,14},{3,7,11,15},{16,20,24,28},{17,21,25,2..., dimensions={0}, use_global_device_ids=true | all-gather | bytes 327680 | tf_op jit(solution)/shard_map/all_gather | solution.py:263
  123.3 0.9 reshape.45
  124.3 3.5 %all-to-all-start.2 = ((bf16[4,128,4,128]{3,2,1,0:T(4,128)(2,1)}), bf16[4,128,4,128]{3,2,1,0:T(4,128)(2,1)S(1)}, u32[]{:S(2)}, u32[]{:S(2)}) async-start(bf16[4,128,4,128]{3,2,1,0:T(4,128)(2,1)} %reshape.45), calls=%async_computation.3 | async-start | bytes 1048576 | tf_op jit(solution)/shard_map/all_to_all | solution.py:225
  128.7 7.9 %all-to-all-done.2 = bf16[4,128,4,128]{3,2,1,0:T(4,128)(2,1)S(1)} async-done(((bf16[4,128,4,128]{3,2,1,0:T(4,128)(2,1)}), bf16[4,128,4,128]{3,2,1,0:T(4,128)(2,1)S(1)}, u32[]{:S(2)}, u32[]{:S(2)}) %all-to-all-start.2) | async-done | bytes 524320 | tf_op jit(solution)/shard_map/all_to_all | solution.py:225
  136.6 3.5 %all-to-all-start.3 = ((bf16[4,128,4,128]{3,2,1,0:T(4,128)(2,1)}), bf16[4,128,4,128]{3,2,1,0:T(4,128)(2,1)S(1)}, u32[]{:S(2)}, u32[]{:S(2)}) async-start(bf16[4,128,4,128]{3,2,1,0:T(4,128)(2,1)} %reshape.47), calls=%async_computation.4 | async-start | bytes 1048576 | tf_op jit(solution)/shard_map/all_to_all | solution.py:225
  140.7 1.2 reshape.46
  141.9 6.9 %all-to-all-done.3 = bf16[4,128,4,128]{3,2,1,0:T(4,128)(2,1)S(1)} async-done(((bf16[4,128,4,128]{3,2,1,0:T(4,128)(2,1)}), bf16[4,128,4,128]{3,2,1,0:T(4,128)(2,1)S(1)}, u32[]{:S(2)}, u32[]{:S(2)}) %all-to-all-start.3) | async-done | bytes 524320 | tf_op jit(solution)/shard_map/all_to_all | solution.py:225
  149.5 1.2 reshape.48
  150.7 2.1 %convert_element_type.11 = f32[128,2048]{1,0:T(8,128)} convert(bf16[128,2048]{1,0:T(8,128)(2,1)} %reduce-scatter.5.cloned.1.call-done) | non-fusion elementwise | flops 262144 | bytes 1572864 | tf_op jit(solution)/shard_map/convert_element_type | solution.py:256
  152.9 20.6 %reduce-scatter.3.cloned.1.call-done = bf16[128,2048]{1,0:T(8,128)(2,1)} async-done(((bf16[512,2048]{1,0:T(8,128)(2,1)}), bf16[128,2048]{1,0:T(8,128)(2,1)}) %reduce-scatter.3.cloned.1.call-update) | async-done | bytes 524304 | tf_op jit(solution)/shard_map/reduce_scatter | solution.py:248
  (33 shorter events, 6.4 us)
Async XLA Ops:
  7.2 24.0 %copy-start = (f32[2048]{0:T(1024)S(1)}, f32[2048]{0:T(1024)}, u32[]{:S(2)}) copy-start(f32[2048]{0:T(1024)} %param.12) | copy-start | bytes 24580
  7.2 8.3 %copy-start.1 = (bf16[128,2048]{1,0:T(8,128)(2,1)S(1)}, bf16[128,2048]{1,0:T(8,128)(2,1)}, u32[]{:S(2)}) copy-start(bf16[128,2048]{1,0:T(8,128)(2,1)} %param.8) | copy-start | bytes 1572868
  7.2 58.5 %all-gather.7.cloned.1.call-start = ((), (), s32[]{:S(2)}) async-start(), calls=%async_computation.8 | async-start | bytes 2621440 | tf_op jit(solution)/shard_map/all_gather | solution.py:229
  7.9 82.7 %all-gather.5.cloned.1.call-start = ((), (), s32[]{:S(2)}) async-start(), calls=%async_computation.6 | async-start | bytes 2621440 | tf_op jit(solution)/shard_map/all_gather | solution.py:228
  11.1 19.4 %copy-start.3 = (f32[16,64]{1,0:T(8,128)S(1)}, f32[16,64]{1,0:T(8,128)}, u32[]{:S(2)}) copy-start(f32[16,64]{1,0:T(8,128)} %param.11) | copy-start | bytes 12292
  11.1 19.6 %copy-start.2 = (f32[2048,64]{0,1:T(8,128)S(1)}, f32[2048,64]{0,1:T(8,128)}, u32[]{:S(2)}) copy-start(f32[2048,64]{0,1:T(8,128)} %param.10) | copy-start | bytes 1572868
  11.1 15.9 %all-to-all-start = ((bf16[4,128,4,128]{3,2,1,0:T(4,128)(2,1)}), bf16[4,128,4,128]{3,2,1,0:T(4,128)(2,1)S(1)}, u32[]{:S(2)}, u32[]{:S(2)}) async-start(bf16[4,128,4,128]{3,2,1,0:T(4,128)(2,1)} %bitcast.34), calls=%async_computation | async-start | bytes 1048576 | tf_op jit(solution)/shard_map/all_to_all | solution.py:220
  27.0 14.2 %all-to-all-start.1 = ((bf16[4,128,4,128]{3,2,1,0:T(4,128)(2,1)}), bf16[4,128,4,128]{3,2,1,0:T(4,128)(2,1)S(1)}, u32[]{:S(2)}, u32[]{:S(2)}) async-start(bf16[4,128,4,128]{3,2,1,0:T(4,128)(2,1)} %bitcast.33), calls=%async_computation.1 | async-start | bytes 1048576 | tf_op jit(solution)/shard_map/all_to_all | solution.py:220
  30.5 120.2 %reduce-scatter.5.cloned.1.call-start = ((), (), s32[]{:S(2)}) async-start(), calls=%async_computation.9 | async-start | bytes 2621440 | tf_op jit(solution)/shard_map/reduce_scatter | solution.py:254
  69.9 103.5 %reduce-scatter.3.cloned.1.call-start = ((), (), s32[]{:S(2)}) async-start(), calls=%async_computation.7 | async-start | bytes 2621440 | tf_op jit(solution)/shard_map/reduce_scatter | solution.py:248
  124.3 12.3 %all-to-all-start.2 = ((bf16[4,128,4,128]{3,2,1,0:T(4,128)(2,1)}), bf16[4,128,4,128]{3,2,1,0:T(4,128)(2,1)S(1)}, u32[]{:S(2)}, u32[]{:S(2)}) async-start(bf16[4,128,4,128]{3,2,1,0:T(4,128)(2,1)} %reshape.45), calls=%async_computation.3 | async-start | bytes 1048576 | tf_op jit(solution)/shard_map/all_to_all | solution.py:225
  136.6 12.3 %all-to-all-start.3 = ((bf16[4,128,4,128]{3,2,1,0:T(4,128)(2,1)}), bf16[4,128,4,128]{3,2,1,0:T(4,128)(2,1)S(1)}, u32[]{:S(2)}, u32[]{:S(2)}) async-start(bf16[4,128,4,128]{3,2,1,0:T(4,128)(2,1)} %reshape.47), calls=%async_computation.4 | async-start | bytes 1048576 | tf_op jit(solution)/shard_map/all_to_all | solution.py:225
Sparse Core Ops, SparseCore 0:
  9.6 29.1 all-gather.6
  40.3 50.2 all-gather.4
  93.0 46.7 reduce-scatter.4
  142.8 30.5 reduce-scatter.2

commit v2 on v1

v2 whole, which is shorter than its diff:
```python
import functools

import jax
import jax.numpy as jnp
from jax import lax
from jax.experimental import pallas as pl
from jax.experimental.pallas import tpu as pltpu
from jax.sharding import PartitionSpec as P

B = 64
F32 = jnp.float32
BF16 = jnp.bfloat16


def dot(a, b):
    return jnp.dot(a, b, preferred_element_type=F32)


def split(a):
    hi = a.astype(BF16)
    return hi, (a - hi.astype(F32)).astype(BF16)


def dot3(a, b):
    ah, al = a
    bh, bl = split(b)
    return dot(ah, bh) + dot(ah, bl) + dot(al, bh)


def iota(shape, dim):
    return lax.broadcasted_iota(jnp.int32, shape, dim).astype(F32)


def local_tables(residue, decay_rate, skip_gain, seq_total, outer, inner, mine):
    width, modes = residue.shape
    groups = decay_rate.shape[0]
    lanes = width // (outer * inner)
    per_group = width // groups // lanes
    pick = lambda a: lax.dynamic_index_in_dim(a, mine, 1, keepdims=False)
    rates = jnp.repeat(decay_rate / seq_total, per_group, axis=0).reshape(outer, inner, modes)
    rate = pick(rates)
    rest = pick(residue.reshape(outer, inner, lanes, modes)).transpose(0, 2, 1)
    skip = pick(skip_gain.reshape(outer, inner, lanes))
    return rate[:, None, :], rate[:, :, None], rest, skip[:, None, :]


def make_taps(row_ref, rest_ref, skip_ref, taps_ref, groups):
    modes = rest_ref.shape[1]
    for g in range(groups):
        lag_pow = jnp.exp(-iota((B, modes), 0) * row_ref[g])
        taps = jnp.dot(
            lag_pow, rest_ref[g], preferred_element_type=F32, precision=lax.Precision.HIGHEST
        )
        first = (lax.broadcasted_iota(jnp.int32, taps.shape, 0) == 0).astype(F32)
        taps_ref[g] = taps + first * skip_ref[g]


def local_part(get, taps_ref, col_ref, inner_ref, ends_ref, pad_ref, g, blocks, back, lanes):
    modes = col_ref.shape[1]
    offs = iota((modes, B), 1)
    powers = jnp.exp(-(offs if back else B - 1.0 - offs) * col_ref[g])
    powers = split(powers)
    zeros = jnp.zeros((8, lanes), F32)
    if back:
        pad_ref[B : B + 8, :] = zeros
    else:
        pad_ref[0:8, :] = zeros

    def body(b, carry):
        x = get(b)
        if x.dtype == BF16:
            ends_ref[g, b] = dot(powers[0], x) + dot(powers[1], x)
        else:
            ends_ref[g, b] = dot3(powers, x)
        xf = x.astype(F32)
        if back:
            pad_ref[0:B, :] = xf
        else:
            pad_ref[8 : B + 8, :] = xf
        acc = [jnp.zeros((8, lanes), F32) for _ in range(B // 8)]
        for low in range(8):
            if low == 0:
                shifted = xf
            elif back:
                shifted = pad_ref[low : B + low, :]
            else:
                shifted = pad_ref[8 - low : B + 8 - low, :]
            for high in range(B // 8):
                k = 8 * high + low
                tap = taps_ref[g, k : k + 1, :]
                for r in range(B // 8 - high):
                    if back:
                        acc[r] = acc[r] + tap * shifted[8 * (r + high) : 8 * (r + high) + 8]
                    else:
                        acc[r + high] = acc[r + high] + tap * shifted[8 * r : 8 * r + 8]
        inner_ref[g, pl.ds(pl.multiple_of(b * B, B), B), :] = jnp.concatenate(acc, axis=0)
        return carry

    lax.fori_loop(0, blocks, body, 0)


def plane_end(ends_ref, col_ref, g, blocks, back):
    step = jnp.exp(-float(B) * col_ref[g])
    total = ends_ref[g, blocks - 1 if back else 0]
    for i in range(1, blocks):
        total = step * total + ends_ref[g, blocks - 1 - i if back else i]
    return total


def finish(state, put, rest_ref, row_ref, col_ref, inner_ref, ends_ref, g, blocks, back):
    modes = col_ref.shape[1]
    offs = iota((B, modes), 0)
    lead = split(jnp.exp(-(B - offs if back else offs + 1.0) * row_ref[g]))
    step = jnp.exp(-float(B) * col_ref[g])
    for i in range(blocks):
        b = blocks - 1 - i if back else i
        cross = dot3(lead, state * rest_ref[g])
        put(b, inner_ref[g, b * B : (b + 1) * B, :] + cross)
        state = step * state + ends_ref[g, b]


def incoming(planes_ref, col_ref, g, outer, here, span, back):
    state = jnp.zeros(planes_ref.shape[2:], F32)
    step = jnp.exp(-float(span) * col_ref[g])
    for i in range(outer - 1):
        e = outer - 1 - i if back else i
        use = e > here if back else e < here
        state = jnp.where(use, step * state + planes_ref[e, g].astype(F32), state)
    return state


INNER = 4


def kernel(
    outer, val_ref, gat_ref, w_ref, cot_ref, row_ref, col_ref, rest_ref, skip_ref,
    out_ref, vgrad_ref, ggrad_ref, wgrad_ref,
    stage_v, stage_g, x, gate, cots, wbuf, taps, inner, ends, conv, mixed, grad, pad,
    end_f, end_b, planes_f, planes_b, got_g, got_v, outp, out_send, out_got,
    dwp, sum_got, sum_send, send_sems, recv_sems,
):
    tokens, width = val_ref.shape
    groups, modes, lanes = rest_ref.shape
    span = tokens * INNER
    blocks = span // B
    per = tokens // B
    me = lax.axis_index("ctx")
    here, mine = me // INNER, lax.rem(me, INNER)
    hi, lo = mine // 2, lax.rem(mine, 2)
    peers = (hi * 2 + 1 - lo, (1 - hi) * 2 + lo, (1 - hi) * 2 + 1 - lo)
    core, side, far = peers
    not_first, not_last = here > 0, here < outer - 1

    spots = {}

    def sem(name, index=0, size=1):
        if name not in spots:
            spots[name] = sum(s for _, s in spots.values()), size
        return spots[name][0] + index

    def rdma(src, dst, name, index, size, plane, q, recv=None):
        spot = sem(name, index, size)
        got = spot if recv is None else sem(recv[0], recv[1], recv[2])
        return pltpu.make_async_remote_copy(
            src_ref=src, dst_ref=dst, send_sem=send_sems.at[spot], recv_sem=recv_sems.at[got],
            device_id={"ctx": plane * INNER + q}, device_id_type=pl.DeviceIdType.MESH,
        )

    barrier = pltpu.get_barrier_semaphore()
    for q in peers:
        pl.semaphore_signal(
            barrier, inc=1, device_id={"ctx": here * INNER + q},
            device_id_type=pl.DeviceIdType.MESH,
        )
    for d in range(1, outer):
        plane = lax.rem(here + d, outer)
        pl.semaphore_signal(
            barrier, inc=1, device_id={"ctx": plane * INNER + mine},
            device_id_type=pl.DeviceIdType.MESH,
        )
    pl.semaphore_wait(barrier, INNER - 1 + outer - 1)

    def w_right(slot, src):
        return rdma(src, wbuf.at[slot], "w_right", slot, outer, here + 1, mine,
                    ("w", slot, outer))

    def w_left(slot, src):
        return rdma(src, wbuf.at[slot], "w_left", slot, outer, here - 1, mine,
                    ("w", slot, outer))

    sem("w", 0, outer)
    pl.when(not_last)(lambda: w_right(here, w_ref).start())
    pl.when(not_first)(lambda: w_left(here, w_ref).start())

    def w_step(k):
        def from_left():
            slot = here - k
            w_right(slot, wbuf.at[slot]).wait_recv()
            pl.when(not_last)(lambda: w_right(slot, wbuf.at[slot]).start())

        def from_right():
            slot = here + k
            w_left(slot, wbuf.at[slot]).wait_recv()
            pl.when(not_first)(lambda: w_left(slot, wbuf.at[slot]).start())

        pl.when(here - k >= 0)(from_left)
        pl.when(here + k < outer)(from_right)

    def to_channels(stage, dst, name, src):
        if src is not None:
            for q in range(INNER):
                for z in range(outer):
                    at = (z * INNER + q) * lanes
                    stage[q, z] = src[:, at : at + lanes]
        copies = [
            rdma(stage.at[q], dst.at[:, mine], name, i, 3, here, q) for i, q in enumerate(peers)
        ]
        if src is not None:
            for c in copies:
                c.start()
            dst[:, pl.ds(mine, 1)] = stage[pl.ds(mine, 1)].reshape(outer, 1, tokens, lanes)
        return copies

    val_copies = to_channels(stage_v, x, "values", val_ref)
    gat_copies = to_channels(stage_g, gate, "gating", gat_ref)
    cot_core = rdma(cot_ref, cots.at[mine], "cot", 0, 3, here, core)
    cot_side = rdma(cot_ref, cots.at[mine], "cot", 1, 3, here, side)
    cot_next = rdma(cots.at[side], cots.at[side], "cot", 2, 3, here, core)
    cot_side.start()
    cot_core.start()
    wbuf[pl.ds(here, 1)] = w_ref[...].reshape(1, w_ref.shape[0], width)
    cots[pl.ds(mine, 1)] = cot_ref[...].reshape(1, tokens, width)

    make_taps(row_ref, rest_ref, skip_ref, taps, groups)
    for c in val_copies:
        c.wait_recv()

    def forward_group(g, carry):
        def get(b):
            return x[g, b // per, pl.ds(pl.multiple_of(lax.rem(b, per) * B, B), B), :]

        local_part(get, taps, col_ref, inner, ends, pad, g, blocks, False, lanes)
        end_f[g] = plane_end(ends, col_ref, g, blocks, False).astype(BF16)
        return carry

    lax.fori_loop(0, groups, forward_group, 0)

    def states(end, planes, name, e, upward):
        return rdma(end, planes.at[here], name, e, outer, e, mine, (name + "_got", here, outer))

    def states_got(end, planes, name, e):
        return rdma(end, planes.at[e], name, e, outer, e, mine, (name + "_got", e, outer))

    def each(planes_of, act):
        for e in range(outer):
            pl.when(planes_of(e))(functools.partial(act, e))

    sem("fwd", 0, outer)
    sem("fwd_got", 0, outer)
    sem("bwd", 0, outer)
    sem("bwd_got", 0, outer)
    later = lambda e: here < e
    earlier = lambda e: here > e
    each(later, lambda e: states(end_f, planes_f, "fwd", e, True).start())
    w_step(1)
    for c in gat_copies:
        c.wait_recv()
    each(earlier, lambda e: states_got(end_f, planes_f, "fwd", e).wait_recv())
    for g in range(groups):
        def put(b, value):
            rows = slice((b % per) * B, (b % per + 1) * B)
            conv[g, b * B : (b + 1) * B, :] = value
            m = (gate[g, b // per, rows, :].astype(F32) * value).astype(BF16)
            mixed[b * B : (b + 1) * B, g * lanes : (g + 1) * lanes] = m

        state = incoming(planes_f, col_ref, g, outer, here, span, False)
        finish(state, put, rest_ref, row_ref, col_ref, inner, ends, g, blocks, False)

    cot_side.wait_recv()
    cot_next.start()
    for k in range(2, outer - 1):
        w_step(k)
    cot_core.wait_recv()
    cot_next.wait_recv()


    for g in range(groups):
        dwp[g] = lax.dot_general(
            mixed[:, g * lanes : (g + 1) * lanes], cots[...].reshape(span, width),
            (((0,), (0,)), ((), ())), preferred_element_type=F32,
        )

    def right_copy(e):
        return rdma(sum_send.at[e], sum_got.at[e + 1], "sum_right", e, outer, here + 1, mine)

    def left_copy(e):
        return rdma(sum_send.at[e], sum_got.at[e], "sum_left", e, outer, here - 1, mine)

    def start_right(e):
        sum_send[e] = dwp[e].astype(BF16)
        right_copy(e).start()

    def start_left(e):
        sum_send[e] = dwp[e].astype(BF16)
        left_copy(e).start()

    def pass_right(e):
        right_copy(e).wait_recv()
        sum_send[e] = (dwp[e] + sum_got[e + 1].astype(F32)).astype(BF16)
        right_copy(e).start()

    def pass_left(e):
        left_copy(e).wait_recv()
        sum_send[e] = (dwp[e] + sum_got[e].astype(F32)).astype(BF16)
        left_copy(e).start()

    for k in range(1, outer):
        pl.when(here == 0)(functools.partial(start_right, outer - k))
        pl.when(here == outer - 1)(functools.partial(start_left, k - 1))

    def sum_step(k):
        e = outer - k
        pl.when(jnp.logical_and(not_first, here < e))(functools.partial(pass_right, e))
        f = k - 1
        pl.when(jnp.logical_and(not_last, here > f))(functools.partial(pass_left, f))

    for c in val_copies + gat_copies:
        c.wait_send()

    def backward_group(g):
        grad[...] = lax.dot_general(
            cots[...].reshape(span, width), wbuf[g], (((1,), (1,)), ((), ())),
            preferred_element_type=F32,
        )

        def get(b):
            rows = pl.ds(pl.multiple_of(b * B, B), B)
            sub = pl.ds(pl.multiple_of(lax.rem(b, per) * B, B), B)
            part = grad[rows, :]
            stage_g[b // per, g, sub, :] = (part * conv[g, rows, :]).astype(BF16)
            return part * gate[g, b // per, sub, :].astype(F32)

        local_part(get, taps, col_ref, inner, ends, pad, g, blocks, True, lanes)
        end_b[g] = plane_end(ends, col_ref, g, blocks, True).astype(BF16)

    backward_group(here)

    def around(k, carry):
        pl.when(k == outer - 1)(lambda: w_step(outer - 1))
        pl.when(here - k >= 0)(lambda: backward_group(here - k))
        pl.when(here + k < outer)(lambda: backward_group(here + k))
        return carry

    lax.fori_loop(1, outer, around, 0)
    each(earlier, lambda e: states(end_b, planes_b, "bwd", e, False).start())

    def to_tokens(buf, got, name):
        return [
            rdma(buf.at[q], got.at[mine], name, i, 3, here, q) for i, q in enumerate(peers)
        ]

    gg_copies = to_tokens(stage_g, got_g, "gate_grad")
    vg_copies = to_tokens(stage_v, got_v, "value_grad")
    for c in gg_copies:
        c.start()

    weight_rows = groups * w_ref.shape[0]
    chunk = min(512, width)

    def out_term(j, carry):
        cols = pl.ds(pl.multiple_of(j * chunk, chunk), chunk)
        part = dot(mixed[...], wbuf[:, :, cols].reshape(weight_rows, chunk))
        outp[:, :, cols] = part.reshape(INNER, tokens, chunk)
        return carry

    lax.fori_loop(0, width // chunk, out_term, 0)
    out_far = rdma(out_send.at[0], out_got.at[0], "out", 0, 3, here, core)
    out_core = rdma(out_send.at[1], out_got.at[1], "out", 1, 3, here, core)
    out_side = rdma(out_send.at[2], out_got.at[2], "out", 2, 3, here, side)
    out_send[0] = outp[far].astype(BF16)
    out_far.start()
    out_send[1] = outp[core].astype(BF16)
    out_core.start()
    out_far.wait_recv()
    out_send[2] = (outp[side] + out_got[0].astype(F32)).astype(BF16)
    out_side.start()

    each(later, lambda e: states_got(end_b, planes_b, "bwd", e).wait_recv())
    for g in range(groups):
        def put(b, value):
            rows = slice((b % per) * B, (b % per + 1) * B)
            stage_v[b // per, g, rows, :] = value.astype(BF16)

        state = incoming(planes_b, col_ref, g, outer, here, span, True)
        finish(state, put, rest_ref, row_ref, col_ref, inner, ends, g, blocks, True)
    for c in vg_copies:
        c.start()
    for k in range(1, outer):
        sum_step(k)

    def collect(buf, got, copies, dst):
        got[pl.ds(mine, 1)] = buf[pl.ds(mine, 1)]
        for c in copies:
            c.wait_recv()
        for q in range(INNER):
            for z in range(outer):
                at = (z * INNER + q) * lanes
                dst[:, at : at + lanes] = got[q, z]

    collect(stage_g, got_g, gg_copies, ggrad_ref)
    out_core.wait_recv()
    out_side.wait_recv()
    out_ref[...] = (
        outp[mine] + out_got[1].astype(F32) + out_got[2].astype(F32)
    ).astype(BF16)
    collect(stage_v, got_v, vg_copies, vgrad_ref)

    wgrad_ref[...] = dwp[here]

    def last_right():
        right_copy(here).wait_recv()
        wgrad_ref[...] += sum_got[here + 1].astype(F32)

    def last_left():
        left_copy(here).wait_recv()
        wgrad_ref[...] += sum_got[here].astype(F32)

    pl.when(not_first)(last_right)
    pl.when(not_last)(last_left)

    for c in gg_copies + vg_copies:
        c.wait_send()
    for c in (cot_core, cot_side, cot_next, out_far, out_core, out_side):
        c.wait_send()
    each(later, lambda e: states(end_f, planes_f, "fwd", e, True).wait_send())
    each(earlier, lambda e: states(end_b, planes_b, "bwd", e, False).wait_send())
    for e in range(outer):
        pl.when(jnp.logical_and(not_last, here >= e))(
            lambda e=e: w_right(e, wbuf.at[e]).wait_send()
        )
        pl.when(jnp.logical_and(not_first, here <= e))(
            lambda e=e: w_left(e, wbuf.at[e]).wait_send()
        )
        pl.when(here < e)(lambda e=e: right_copy(e).wait_send())
        pl.when(here > e)(lambda e=e: left_copy(e).wait_send())
    assert sum(s for _, s in spots.values()) <= send_sems.shape[0]


def per_device(values, gating, out_weight, residue, decay_rate, skip_gain, cotangent):
    tokens, width = values.shape
    ctx = lax.axis_size("ctx")
    outer = ctx // INNER
    modes = decay_rate.shape[1]
    lanes = width // ctx
    rows = out_weight.shape[0]
    span = tokens * INNER
    mine = lax.axis_index("ctx") % INNER
    row, col, rest, skip = local_tables(
        residue, decay_rate, skip_gain, float(tokens * ctx), outer, INNER, mine
    )
    quarter = (INNER, outer, tokens, lanes)
    chans = (outer, INNER, tokens, lanes)
    state = (outer, modes, lanes)
    slots = (outer, rows, width)
    scratch = [
        (quarter, BF16), (quarter, BF16), (chans, BF16), (chans, BF16),
        ((INNER, tokens, width), BF16), (slots, BF16), ((outer, B, lanes), F32),
        ((outer, span, lanes), F32), ((outer, span // B, modes, lanes), F32),
        ((outer, span, lanes), F32), ((span, outer * lanes), BF16), ((span, lanes), F32), ((B + 8, lanes), F32),
        (state, BF16), (state, BF16), ((outer,) + state, BF16), ((outer,) + state, BF16),
        (quarter, BF16), (quarter, BF16),
        ((INNER, tokens, width), F32), ((3, tokens, width), BF16), ((3, tokens, width), BF16),
        (slots, F32), ((outer + 1, rows, width), BF16), (slots, BF16),
    ]
    sems = pltpu.SemaphoreType.DMA((18 + 9 * outer,))
    args = (values, gating, out_weight, cotangent, row, col, rest, skip)
    out = jax.ShapeDtypeStruct((tokens, width), BF16)
    macs = 3 * span * outer * lanes * width
    return pl.pallas_call(
        functools.partial(kernel, outer),
        out_shape=[out, out, out, jax.ShapeDtypeStruct((rows, width), F32)],
        in_specs=[pl.BlockSpec(memory_space=pltpu.VMEM)] * len(args),
        out_specs=[pl.BlockSpec(memory_space=pltpu.VMEM)] * 4,
        scratch_shapes=[pltpu.VMEM(s, d) for s, d in scratch] + [sems, sems],
        compiler_params=pltpu.CompilerParams(
            collective_id=0, has_side_effects=True, vmem_limit_bytes=61 * 2**20
        ),
        cost_estimate=pl.CostEstimate(
            flops=2 * macs, bytes_accessed=6 * 2**20, transcendentals=0
        ),
    )(*args)


def solution(mesh):
    rows = P(("parts", "ctx"), None)
    return jax.shard_map(
        per_device,
        mesh=mesh,
        in_specs=(rows, rows, rows, P("parts", None), P("parts", None), P("parts"), rows),
        out_specs=(rows,) * 4,
        check_vma=False,
    )
```

time: 181 us -> 127 us (0.70)
  Pallas kernels: 15.4 us -> 118 us
  waiting for transfers between devices: 77.5 us -> 0 us
  blocking collectives: 33.9 us -> 0 us
  starting transfers between devices: 15 us -> 0 us
  between operations: 14 us -> 0.71 us
  matrix products: 12 us -> 0 us
  other arithmetic: 2.14 us -> 0.01 us
    pallas_call x4 -> x1, Pallas kernels: 15.4 us -> 118 us  [per_device(): pl.pallas_call(functools.partial(kernel, outer), out_shape=[out, out, out...]
    all_to_all x4 -> x0, waiting for transfers between devices: 34.8 us -> none  [the longest x2 20 us: to_channels(): a = lax.all_to_all(a, 'ctx', 0, 0, axis_index_groups=planes, tiled=True)]
    all_gather x2 -> x0, blocking collectives: 33.9 us -> none  [the longest x1 17.4 us: per_device(): planes_f = lax.all_gather(end_f, 'ctx', axis_index_groups=lines)]
    all_gather x2 -> x0, waiting for transfers between devices: 20.7 us -> none  [the longest x1 20.7 us: per_device(): lax.all_gather(out_weight, 'ctx', axis=0, tiled=True, axis_index_groups=l...]
    reduce_scatter x2 -> x0, waiting for transfers between devices: 20.6 us -> none  [the longest x1 20.6 us: per_device(): lax.psum_scatter(partial, 'ctx', scatter_dimension=0, tiled=True, axis_in...]
    all_to_all x4 -> x0, starting transfers between devices: 14.8 us -> none  [the longest x2 7.85 us: to_channels(): a = lax.all_to_all(a, 'ctx', 0, 0, axis_index_groups=planes, tiled=True)]
    dot_general x3 -> x0, matrix products: 12 us -> none  [the longest x1 4.27 us: per_device(): lax.dot_general(mixed, cot, (((0,), (0,)), ((), ())), preferred_element_t...]
    reshape x8 -> x0, local copies, waits for them, and re-layouts: 7.96 us -> none  [the longest x4 3.76 us: to_channels(): a = a.reshape(tokens, outer, inner, lanes).transpose(2, 0, 1, 3)]
  transfers between devices with their start and end apart: 8 -> 0, of which waited for: 6 -> 0; matrix products, arithmetic and copies ran while one was open for 13% -> 0% of each run, Pallas kernels for 9% -> 0%
where the time goes in v2:
time: 127 us
  Pallas kernels  118 us (93%)
  local copies, waits for them, and re-layouts  8.76 us (7%)
    pallas_call x1, Pallas kernels, per_device(): pl.pallas_call(functools.partial(kernel, outer), out_shape=[out, out, out...  118 us
    unnamed x17, local copies, waits for them, and re-layouts  5.88 us

profile of v2, /device:TPU:0, one launch (start us, length us, event | category | flops | bytes accessed | tf_op | source)
XLA Modules:
  0.0 127.2 jit_solution(2263320442734528917)
XLA Ops:
  0.6 0.0 copy-start
  0.7 0.0 copy-start.5
  0.7 0.7 copy-done
  1.3 0.6 constant_dynamic-slice_fusion.skip_ref
  1.9 0.0 copy-done.5
  1.9 0.0 copy-start.4
  1.9 0.8 copy.13.col_ref
  2.7 0.0 copy-done.4
  2.7 1.4 %reshape.15 = f32[4,4,128,64]{2,1,0,3:T(4,128)S(1)} reshape(f32[2048,64]{0,1:T(8,128)} %param.10) | data formatting | bytes 1048576 | tf_op jit(solution)/shard_map/reshape | solution.py:42
  4.1 0.1 constant_dynamic-slice_fusion.1
  4.2 0.7 copy.16
  4.9 117.8 %shard_map.102 = (bf16[128,2048]{1,0:T(8,128)(2,1)}, bf16[128,2048]{1,0:T(8,128)(2,1)}, bf16[128,2048]{1,0:T(8,128)(2,1)}, f32[128,2048]{1,0:T(8,128)}) custom-call(bf16[128,2048]{1,0:T(8,128)(2,1)} %val_ref.1, bf16[128,2048]{1,0:T(8,128)(2,1)} %gat_ref.1, bf16[128,2048]{1,0:T(8,128)(2,1)} %w_ref.1, bf16[128,2048]{1,0:T(8,128)(2,1)} %cot_ref.1, ...), custom_call_target="tpu_custom_call" | custom-call | flops 3221225472 | bytes 6291456 | tf_op jit(solution)/shard_map/pallas_call | solution.py:479
  122.7 0.0 copy-start.3
  122.7 0.0 copy-start.2
  122.7 2.0 %copy.21 = bf16[128,2048]{1,0:T(8,128)(2,1)} copy(bf16[128,2048]{1,0:T(8,128)(2,1)} %get-tuple-element.8) | data formatting | bytes 1048576
  124.7 0.0 copy-done.3
  124.7 0.0 copy-start.1
  124.7 0.8 copy.22
  125.5 0.0 copy-done.2
  125.5 0.8 copy.23
  126.3 0.0 copy-done.1
  126.3 1.0 copy.24
  (2 shorter events, 0.0 us)
Async XLA Ops:
  0.6 0.7 copy-start
  0.7 1.3 copy-start.5
  1.9 0.8 copy-start.4
  122.7 2.0 %copy-start.3 = (bf16[128,2048]{1,0:T(8,128)(2,1)S(1)}, bf16[128,2048]{1,0:T(8,128)(2,1)}, u32[]{:S(2)}) copy-start(bf16[128,2048]{1,0:T(8,128)(2,1)} %get-tuple-element.9) | copy-start | bytes 1572868
  122.7 2.8 %copy-start.2 = (bf16[128,2048]{1,0:T(8,128)(2,1)S(1)}, bf16[128,2048]{1,0:T(8,128)(2,1)}, u32[]{:S(2)}) copy-start(bf16[128,2048]{1,0:T(8,128)(2,1)} %get-tuple-element.10) | copy-start | bytes 1572868
  124.7 1.6 %copy-start.1 = (f32[128,2048]{1,0:T(8,128)S(1)}, f32[128,2048]{1,0:T(8,128)}, u32[]{:S(2)}) copy-start(f32[128,2048]{1,0:T(8,128)} %get-tuple-element.11) | copy-start | bytes 3145732

commit v3 on v2

--- a/solution.py
+++ b/solution.py
@@ -31,34 +31,28 @@
     return lax.broadcasted_iota(jnp.int32, shape, dim).astype(F32)
 
 
-def local_tables(residue, decay_rate, skip_gain, seq_total, outer, inner, mine):
-    width, modes = residue.shape
-    groups = decay_rate.shape[0]
-    lanes = width // (outer * inner)
-    per_group = width // groups // lanes
-    pick = lambda a: lax.dynamic_index_in_dim(a, mine, 1, keepdims=False)
-    rates = jnp.repeat(decay_rate / seq_total, per_group, axis=0).reshape(outer, inner, modes)
-    rate = pick(rates)
-    rest = pick(residue.reshape(outer, inner, lanes, modes)).transpose(0, 2, 1)
-    skip = pick(skip_gain.reshape(outer, inner, lanes))
-    return rate[:, None, :], rate[:, :, None], rest, skip[:, None, :]
-
-
-def make_taps(row_ref, rest_ref, skip_ref, taps_ref, groups):
-    modes = rest_ref.shape[1]
-    for g in range(groups):
+def make_tables(
+    res_ref, rate_ref, skip_ref, row_ref, col_ref, rest_ref, taps_ref, seq_total, outer, mine
+):
+    _, modes, lanes = rest_ref.shape
+    for g in range(outer):
+        block = g * INNER + mine
+        group = block * rate_ref.shape[0] // (outer * INNER)
+        row_ref[g] = rate_ref[pl.ds(group, 1), :] / seq_total
+        col_ref[g] = jnp.broadcast_to(row_ref[g], (128, modes)).T
+        rest_ref[g] = res_ref[pl.ds(pl.multiple_of(block * lanes, lanes), lanes), :].T
         lag_pow = jnp.exp(-iota((B, modes), 0) * row_ref[g])
         taps = jnp.dot(
             lag_pow, rest_ref[g], preferred_element_type=F32, precision=lax.Precision.HIGHEST
         )
         first = (lax.broadcasted_iota(jnp.int32, taps.shape, 0) == 0).astype(F32)
-        taps_ref[g] = taps + first * skip_ref[g]
+        taps_ref[g] = taps + first * skip_ref[pl.ds(block, 1), :]
 
 
 def local_part(get, taps_ref, col_ref, inner_ref, ends_ref, pad_ref, g, blocks, back, lanes):
     modes = col_ref.shape[1]
     offs = iota((modes, B), 1)
-    powers = jnp.exp(-(offs if back else B - 1.0 - offs) * col_ref[g])
+    powers = jnp.exp(-(offs if back else B - 1.0 - offs) * col_ref[g][:, :B])
     powers = split(powers)
     zeros = jnp.zeros((8, lanes), F32)
     if back:
@@ -100,8 +94,8 @@
 
 
 def plane_end(ends_ref, col_ref, g, blocks, back):
-    step = jnp.exp(-float(B) * col_ref[g])
     total = ends_ref[g, blocks - 1 if back else 0]
+    step = jnp.exp(-float(B) * col_ref[g][:, : total.shape[1]])
     for i in range(1, blocks):
         total = step * total + ends_ref[g, blocks - 1 - i if back else i]
     return total
@@ -111,7 +105,7 @@
     modes = col_ref.shape[1]
     offs = iota((B, modes), 0)
     lead = split(jnp.exp(-(B - offs if back else offs + 1.0) * row_ref[g]))
-    step = jnp.exp(-float(B) * col_ref[g])
+    step = jnp.exp(-float(B) * col_ref[g][:, : state.shape[1]])
     for i in range(blocks):
         b = blocks - 1 - i if back else i
         cross = dot3(lead, state * rest_ref[g])
@@ -121,7 +115,7 @@
 
 def incoming(planes_ref, col_ref, g, outer, here, span, back):
     state = jnp.zeros(planes_ref.shape[2:], F32)
-    step = jnp.exp(-float(span) * col_ref[g])
+    step = jnp.exp(-float(span) * col_ref[g][:, : state.shape[1]])
     for i in range(outer - 1):
         e = outer - 1 - i if back else i
         use = e > here if back else e < here
@@ -133,9 +127,9 @@
 
 
 def kernel(
-    outer, val_ref, gat_ref, w_ref, cot_ref, row_ref, col_ref, rest_ref, skip_ref,
+    outer, val_ref, gat_ref, w_ref, cot_ref, res_ref, rate_ref, skip_ref,
     out_ref, vgrad_ref, ggrad_ref, wgrad_ref,
-    stage_v, stage_g, x, gate, cots, wbuf, taps, inner, ends, conv, mixed, grad, pad,
+    row_ref, col_ref, rest_ref, stage_v, stage_g, x, gate, cots, wbuf, taps, inner, ends, conv, mixed, grad, pad,
     end_f, end_b, planes_f, planes_b, got_g, got_v, outp, out_send, out_got,
     dwp, sum_got, sum_send, send_sems, recv_sems,
 ):
@@ -222,18 +216,21 @@
         return copies
 
     val_copies = to_channels(stage_v, x, "values", val_ref)
-    gat_copies = to_channels(stage_g, gate, "gating", gat_ref)
     cot_core = rdma(cot_ref, cots.at[mine], "cot", 0, 3, here, core)
     cot_side = rdma(cot_ref, cots.at[mine], "cot", 1, 3, here, side)
     cot_next = rdma(cots.at[side], cots.at[side], "cot", 2, 3, here, core)
-    cot_side.start()
     cot_core.start()
+    make_tables(
+        res_ref, rate_ref, skip_ref, row_ref, col_ref, rest_ref, taps,
+        float(tokens * outer * INNER), outer, mine,
+    )
+    gat_copies = to_channels(stage_g, gate, "gating", gat_ref)
     wbuf[pl.ds(here, 1)] = w_ref[...].reshape(1, w_ref.shape[0], width)
     cots[pl.ds(mine, 1)] = cot_ref[...].reshape(1, tokens, width)
 
-    make_taps(row_ref, rest_ref, skip_ref, taps, groups)
     for c in val_copies:
         c.wait_recv()
+    cot_side.start()
 
     def forward_group(g, carry):
         def get(b):
@@ -284,12 +281,6 @@
     cot_next.wait_recv()
 
 
-    for g in range(groups):
-        dwp[g] = lax.dot_general(
-            mixed[:, g * lanes : (g + 1) * lanes], cots[...].reshape(span, width),
-            (((0,), (0,)), ((), ())), preferred_element_type=F32,
-        )
-
     def right_copy(e):
         return rdma(sum_send.at[e], sum_got.at[e + 1], "sum_right", e, outer, here + 1, mine)
 
@@ -314,15 +305,26 @@
         sum_send[e] = (dwp[e] + sum_got[e].astype(F32)).astype(BF16)
         left_copy(e).start()
 
-    for k in range(1, outer):
-        pl.when(here == 0)(functools.partial(start_right, outer - k))
-        pl.when(here == outer - 1)(functools.partial(start_left, k - 1))
-
-    def sum_step(k):
-        e = outer - k
-        pl.when(jnp.logical_and(not_first, here < e))(functools.partial(pass_right, e))
-        f = k - 1
-        pl.when(jnp.logical_and(not_last, here > f))(functools.partial(pass_left, f))
+    def weight_terms(order, end, start):
+        for g in order:
+            dwp[g] = lax.dot_general(
+                mixed[:, g * lanes : (g + 1) * lanes], cots[...].reshape(span, width),
+                (((0,), (0,)), ((), ())), preferred_element_type=F32,
+            )
+            if g != end:
+                pl.when(here == end)(functools.partial(start, g))
+
+    lower = here < outer // 2
+    upper = here >= outer // 2
+    pl.when(lower)(lambda: weight_terms(range(outer)[::-1], 0, start_right))
+    pl.when(upper)(lambda: weight_terms(range(outer), outer - 1, start_left))
+
+    def sum_step(k, near):
+        e, f = outer - k, k - 1
+        right = jnp.logical_and(not_first, here < e)
+        left = jnp.logical_and(not_last, here > f)
+        pl.when(jnp.logical_and(lower if near else upper, right))(functools.partial(pass_right, e))
+        pl.when(jnp.logical_and(upper if near else lower, left))(functools.partial(pass_left, f))
 
     for c in val_copies + gat_copies:
         c.wait_send()
@@ -363,6 +365,7 @@
     vg_copies = to_tokens(stage_v, got_v, "value_grad")
     for c in gg_copies:
         c.start()
+    sum_step(1, True)
 
     weight_rows = groups * w_ref.shape[0]
     chunk = min(512, width)
@@ -395,8 +398,10 @@
         finish(state, put, rest_ref, row_ref, col_ref, inner, ends, g, blocks, True)
     for c in vg_copies:
         c.start()
+    for k in range(2, outer):
+        sum_step(k, True)
     for k in range(1, outer):
-        sum_step(k)
+        sum_step(k, False)
 
     def collect(buf, got, copies, dst):
         got[pl.ds(mine, 1)] = buf[pl.ds(mine, 1)]
@@ -454,15 +459,12 @@
     lanes = width // ctx
     rows = out_weight.shape[0]
     span = tokens * INNER
-    mine = lax.axis_index("ctx") % INNER
-    row, col, rest, skip = local_tables(
-        residue, decay_rate, skip_gain, float(tokens * ctx), outer, INNER, mine
-    )
     quarter = (INNER, outer, tokens, lanes)
     chans = (outer, INNER, tokens, lanes)
     state = (outer, modes, lanes)
     slots = (outer, rows, width)
     scratch = [
+        ((outer, 1, modes), F32), ((outer, modes, 128), F32), (state, F32),
         (quarter, BF16), (quarter, BF16), (chans, BF16), (chans, BF16),
         ((INNER, tokens, width), BF16), (slots, BF16), ((outer, B, lanes), F32),
         ((outer, span, lanes), F32), ((outer, span // B, modes, lanes), F32),
@@ -473,7 +475,7 @@
         (slots, F32), ((outer + 1, rows, width), BF16), (slots, BF16),
     ]
     sems = pltpu.SemaphoreType.DMA((18 + 9 * outer,))
-    args = (values, gating, out_weight, cotangent, row, col, rest, skip)
+    args = (values, gating, out_weight, cotangent, residue, decay_rate, skip_gain.reshape(ctx, lanes))
     out = jax.ShapeDtypeStruct((tokens, width), BF16)
     macs = 3 * span * outer * lanes * width
     return pl.pallas_call(

time: 127 us -> 99.8 us (0.79)
  Pallas kernels: 118 us -> 92.1 us
  local copies, waits for them, and re-layouts: 8.76 us -> 6.89 us
    pallas_call x1, Pallas kernels: 118 us -> 92.1 us  [per_device(): pl.pallas_call(functools.partial(kernel, outer), out_shape=[out, out, out...]
    reshape x1 -> x0, local copies, waits for them, and re-layouts: 1.39 us -> none  [local_tables(): rest = pick(residue.reshape(outer, inner, lanes, modes)).transpose(0, 2, 1)]
    unnamed x17 -> x11, local copies, waits for them, and re-layouts: 5.88 us -> 6.89 us
where the time goes in v3:
time: 99.8 us; the launch traced here: 99.6 us
  Pallas kernels  92.1 us (92%)
  local copies, waits for them, and re-layouts  6.89 us (7%)
    pallas_call x1, Pallas kernels, per_device(): pl.pallas_call(functools.partial(kernel, outer), out_shape=[out, out, out...  92.1 us
    unnamed x11, local copies, waits for them, and re-layouts  6.89 us

profile of v3, /device:TPU:0, one launch (start us, length us, event | category | flops | bytes accessed | tf_op | source)
XLA Modules:
  0.0 99.6 jit_solution(6451221207633063071)
XLA Ops:
  0.6 2.4 %copy.11.res_ref = f32[2048,64]{1,0:T(8,128)} copy(f32[2048,64]{0,1:T(8,128)} %param.10) | data formatting | bytes 1048576 | tf_op args[3]
  3.0 92.1 %shard_map.102 = (bf16[128,2048]{1,0:T(8,128)(2,1)}, bf16[128,2048]{1,0:T(8,128)(2,1)}, bf16[128,2048]{1,0:T(8,128)(2,1)}, f32[128,2048]{1,0:T(8,128)}) custom-call(bf16[128,2048]{1,0:T(8,128)(2,1)} %val_ref.1, bf16[128,2048]{1,0:T(8,128)(2,1)} %gat_ref.1, bf16[128,2048]{1,0:T(8,128)(2,1)} %w_ref.1, bf16[128,2048]{1,0:T(8,128)(2,1)} %cot_ref.1, ...), custom_call_target="tpu_custom_call" | custom-call | flops 3221225472 | bytes 6291456 | tf_op jit(solution)/shard_map/pallas_call | solution.py:481
  95.1 0.0 copy-start.2
  95.1 0.0 copy-start.1
  95.1 2.0 %copy.16 = bf16[128,2048]{1,0:T(8,128)(2,1)} copy(bf16[128,2048]{1,0:T(8,128)(2,1)} %get-tuple-element.8) | data formatting | bytes 1048576
  97.1 0.0 copy-done.2
  97.1 0.0 copy-start
  97.1 0.8 copy.17
  97.9 0.0 copy-done.1
  97.9 0.8 copy.18
  98.7 0.0 copy-done
  98.7 1.0 copy.19
Async XLA Ops:
  95.1 2.0 %copy-start.2 = (bf16[128,2048]{1,0:T(8,128)(2,1)S(1)}, bf16[128,2048]{1,0:T(8,128)(2,1)}, u32[]{:S(2)}) copy-start(bf16[128,2048]{1,0:T(8,128)(2,1)} %get-tuple-element.9) | copy-start | bytes 1572868
  95.1 2.8 %copy-start.1 = (bf16[128,2048]{1,0:T(8,128)(2,1)S(1)}, bf16[128,2048]{1,0:T(8,128)(2,1)}, u32[]{:S(2)}) copy-start(bf16[128,2048]{1,0:T(8,128)(2,1)} %get-tuple-element.10) | copy-start | bytes 1572868
  97.1 1.6 %copy-start = (f32[128,2048]{1,0:T(8,128)S(1)}, f32[128,2048]{1,0:T(8,128)}, u32[]{:S(2)}) copy-start(f32[128,2048]{1,0:T(8,128)} %get-tuple-element.11) | copy-start | bytes 3145732

commit v4 on v3

--- a/solution.py
+++ b/solution.py
@@ -40,7 +40,11 @@
         group = block * rate_ref.shape[0] // (outer * INNER)
         row_ref[g] = rate_ref[pl.ds(group, 1), :] / seq_total
         col_ref[g] = jnp.broadcast_to(row_ref[g], (128, modes)).T
-        rest_ref[g] = res_ref[pl.ds(pl.multiple_of(block * lanes, lanes), lanes), :].T
+        chans = pl.ds(pl.multiple_of(block * lanes, lanes), lanes)
+        if res_ref.shape[0] == modes:
+            rest_ref[g] = res_ref[:, chans]
+        else:
+            rest_ref[g] = res_ref[chans, :].T
         lag_pow = jnp.exp(-iota((B, modes), 0) * row_ref[g])
         taps = jnp.dot(
             lag_pow, rest_ref[g], preferred_element_type=F32, precision=lax.Precision.HIGHEST
@@ -49,16 +53,11 @@
         taps_ref[g] = taps + first * skip_ref[pl.ds(block, 1), :]
 
 
-def local_part(get, taps_ref, col_ref, inner_ref, ends_ref, pad_ref, g, blocks, back, lanes):
+def ends_part(get, col_ref, ends_ref, g, blocks, back):
     modes = col_ref.shape[1]
     offs = iota((modes, B), 1)
     powers = jnp.exp(-(offs if back else B - 1.0 - offs) * col_ref[g][:, :B])
     powers = split(powers)
-    zeros = jnp.zeros((8, lanes), F32)
-    if back:
-        pad_ref[B : B + 8, :] = zeros
-    else:
-        pad_ref[0:8, :] = zeros
 
     def body(b, carry):
         x = get(b)
@@ -66,7 +65,20 @@
             ends_ref[g, b] = dot(powers[0], x) + dot(powers[1], x)
         else:
             ends_ref[g, b] = dot3(powers, x)
-        xf = x.astype(F32)
+        return carry
+
+    lax.fori_loop(0, blocks, body, 0)
+
+
+def inner_part(get, taps_ref, inner_ref, pad_ref, g, blocks, back, lanes):
+    zeros = jnp.zeros((8, lanes), F32)
+    if back:
+        pad_ref[B : B + 8, :] = zeros
+    else:
+        pad_ref[0:8, :] = zeros
+
+    def body(b, carry):
+        xf = get(b).astype(F32)
         if back:
             pad_ref[0:B, :] = xf
         else:
@@ -232,15 +244,18 @@
         c.wait_recv()
     cot_side.start()
 
-    def forward_group(g, carry):
+    def forward_group(inside, g, carry):
         def get(b):
             return x[g, b // per, pl.ds(pl.multiple_of(lax.rem(b, per) * B, B), B), :]
 
-        local_part(get, taps, col_ref, inner, ends, pad, g, blocks, False, lanes)
-        end_f[g] = plane_end(ends, col_ref, g, blocks, False).astype(BF16)
+        if inside:
+            inner_part(get, taps, inner, pad, g, blocks, False, lanes)
+        else:
+            ends_part(get, col_ref, ends, g, blocks, False)
+            end_f[g] = plane_end(ends, col_ref, g, blocks, False).astype(BF16)
         return carry
 
-    lax.fori_loop(0, groups, forward_group, 0)
+    lax.fori_loop(0, groups, functools.partial(forward_group, False), 0)
 
     def states(end, planes, name, e, upward):
         return rdma(end, planes.at[here], name, e, outer, e, mine, (name + "_got", here, outer))
@@ -259,6 +274,7 @@
     later = lambda e: here < e
     earlier = lambda e: here > e
     each(later, lambda e: states(end_f, planes_f, "fwd", e, True).start())
+    lax.fori_loop(0, groups, functools.partial(forward_group, True), 0)
     w_step(1)
     for c in gat_copies:
         c.wait_recv()
@@ -340,10 +356,20 @@
             sub = pl.ds(pl.multiple_of(lax.rem(b, per) * B, B), B)
             part = grad[rows, :]
             stage_g[b // per, g, sub, :] = (part * conv[g, rows, :]).astype(BF16)
-            return part * gate[g, b // per, sub, :].astype(F32)
-
-        local_part(get, taps, col_ref, inner, ends, pad, g, blocks, True, lanes)
+            signal_back = part * gate[g, b // per, sub, :].astype(F32)
+            inner[g, rows, :] = signal_back
+            return signal_back
+
+        ends_part(get, col_ref, ends, g, blocks, True)
         end_b[g] = plane_end(ends, col_ref, g, blocks, True).astype(BF16)
+        each(earlier, lambda e: rdma(
+            end_b.at[g], planes_b.at[here, g], "bwd", e, outer, e, mine, ("bwd_got", here, outer)
+        ).start())
+
+        def again(b):
+            return inner[g, pl.ds(pl.multiple_of(b * B, B), B), :]
+
+        inner_part(again, taps, inner, pad, g, blocks, True, lanes)
 
     backward_group(here)
 
@@ -351,11 +377,10 @@
         pl.when(k == outer - 1)(lambda: w_step(outer - 1))
         pl.when(here - k >= 0)(lambda: backward_group(here - k))
         pl.when(here + k < outer)(lambda: backward_group(here + k))
+        pl.when(k == 1)(lambda: sum_step(1, True))
         return carry
 
     lax.fori_loop(1, outer, around, 0)
-    each(earlier, lambda e: states(end_b, planes_b, "bwd", e, False).start())
-
     def to_tokens(buf, got, name):
         return [
             rdma(buf.at[q], got.at[mine], name, i, 3, here, q) for i, q in enumerate(peers)
@@ -365,7 +390,6 @@
     vg_copies = to_tokens(stage_v, got_v, "value_grad")
     for c in gg_copies:
         c.start()
-    sum_step(1, True)
 
     weight_rows = groups * w_ref.shape[0]
     chunk = min(512, width)
@@ -384,6 +408,8 @@
     out_far.start()
     out_send[1] = outp[core].astype(BF16)
     out_core.start()
+    for k in range(2, outer):
+        sum_step(k, True)
     out_far.wait_recv()
     out_send[2] = (outp[side] + out_got[0].astype(F32)).astype(BF16)
     out_side.start()
@@ -398,8 +424,6 @@
         finish(state, put, rest_ref, row_ref, col_ref, inner, ends, g, blocks, True)
     for c in vg_copies:
         c.start()
-    for k in range(2, outer):
-        sum_step(k, True)
     for k in range(1, outer):
         sum_step(k, False)
 
@@ -475,10 +499,11 @@
         (slots, F32), ((outer + 1, rows, width), BF16), (slots, BF16),
     ]
     sems = pltpu.SemaphoreType.DMA((18 + 9 * outer,))
-    args = (values, gating, out_weight, cotangent, residue, decay_rate, skip_gain.reshape(ctx, lanes))
+    table = residue.T if lanes % 128 == 0 else residue
+    args = (values, gating, out_weight, cotangent, table, decay_rate, skip_gain.reshape(ctx, lanes))
     out = jax.ShapeDtypeStruct((tokens, width), BF16)
     macs = 3 * span * outer * lanes * width
-    return pl.pallas_call(
+    results = pl.pallas_call(
         functools.partial(kernel, outer),
         out_shape=[out, out, out, jax.ShapeDtypeStruct((rows, width), F32)],
         in_specs=[pl.BlockSpec(memory_space=pltpu.VMEM)] * len(args),
@@ -491,6 +516,24 @@
             flops=2 * macs, bytes_accessed=6 * 2**20, transcendentals=0
         ),
     )(*args)
+    whole = [pl.BlockSpec(memory_space=pltpu.HBM)] * 4
+    return pl.pallas_call(
+        hand_over,
+        out_shape=[jax.ShapeDtypeStruct(r.shape, r.dtype) for r in results],
+        in_specs=whole,
+        out_specs=whole,
+        scratch_shapes=[pltpu.SemaphoreType.DMA((4,))],
+    )(*results)
+
+
+def hand_over(*refs):
+    copies = [
+        pltpu.make_async_copy(refs[i], refs[4 + i], refs[8].at[i]) for i in range(4)
+    ]
+    for c in copies:
+        c.start()
+    for c in copies:
+        c.wait()
 
 
 def solution(mesh):

time: 99.8 us -> 173 us (1.73)
  Pallas kernels: 92.1 us -> 173 us
  local copies, waits for them, and re-layouts: 6.89 us -> 0 us
    pallas_call x0 -> x1, Pallas kernels: none -> 80.5 us  [per_device(): pl.pallas_call(hand_over, out_shape=[jax.ShapeDtypeStruct(r.shape, r.dtyp...]
    unnamed x11 -> x0, local copies, waits for them, and re-layouts: 6.89 us -> none
where the time goes in v4:
time: 173 us
  Pallas kernels  173 us (100%)
    pallas_call x1, Pallas kernels, per_device(): pl.pallas_call(functools.partial(kernel, outer), out_shape=[out, out, out...  92.1 us
    pallas_call x1, Pallas kernels, per_device(): pl.pallas_call(hand_over, out_shape=[jax.ShapeDtypeStruct(r.shape, r.dtyp...  80.5 us

profile of v4, /device:TPU:0, one launch (start us, length us, event | category | flops | bytes accessed | tf_op | source)
XLA Modules:
  0.0 173.3 jit_solution(583114929538957108)
XLA Ops:
  0.6 92.1 %shard_map.102 = (bf16[128,2048]{1,0:T(8,128)(2,1)}, bf16[128,2048]{1,0:T(8,128)(2,1)}, bf16[128,2048]{1,0:T(8,128)(2,1)}, f32[128,2048]{1,0:T(8,128)}) custom-call(bf16[128,2048]{1,0:T(8,128)(2,1)} %val_ref.1, bf16[128,2048]{1,0:T(8,128)(2,1)} %gat_ref.1, bf16[128,2048]{1,0:T(8,128)(2,1)} %w_ref.1, bf16[128,2048]{1,0:T(8,128)(2,1)} %cot_ref.1, ...), custom_call_target="tpu_custom_call" | custom-call | flops 3221225472 | bytes 6291456 | tf_op jit(solution)/shard_map/pallas_call | solution.py:506
  92.7 80.5 %shard_map.103 = (bf16[128,2048]{1,0:T(8,128)(2,1)}, bf16[128,2048]{1,0:T(8,128)(2,1)}, bf16[128,2048]{1,0:T(8,128)(2,1)}, f32[128,2048]{1,0:T(8,128)}) custom-call(bf16[128,2048]{1,0:T(8,128)(2,1)} %get-tuple-element.8.refs_0_, bf16[128,2048]{1,0:T(8,128)(2,1)} %get-tuple-element.9.refs_1_, bf16[128,2048]{1,0:T(8,128)(2,1)} %get-tuple-element.10.refs_2_, ...), custom_call_target="tpu_custom_call" | custom-call | tf_op jit(solution)/shard_map/pallas_call | solution.py:520

commit v5 on v4

--- a/solution.py
+++ b/solution.py
@@ -228,9 +228,17 @@
         return copies
 
     val_copies = to_channels(stage_v, x, "values", val_ref)
-    cot_core = rdma(cot_ref, cots.at[mine], "cot", 0, 3, here, core)
-    cot_side = rdma(cot_ref, cots.at[mine], "cot", 1, 3, here, side)
-    cot_next = rdma(cots.at[side], cots.at[side], "cot", 2, 3, here, core)
+    cot_core = rdma(cot_ref, cots.at[mine], "cot", 0, 1, here, core)
+    half = width // 2
+    halves = [slice(h * half, (h + 1) * half) for h in range(2)]
+    cot_side = [
+        rdma(cot_ref.at[:, c], cots.at[mine, :, c], "cot_side", h, 2, here, side)
+        for h, c in enumerate(halves)
+    ]
+    cot_next = [
+        rdma(cots.at[side, :, c], cots.at[side, :, c], "cot_next", h, 2, here, core)
+        for h, c in enumerate(halves)
+    ]
     cot_core.start()
     make_tables(
         res_ref, rate_ref, skip_ref, row_ref, col_ref, rest_ref, taps,
@@ -242,7 +250,7 @@
 
     for c in val_copies:
         c.wait_recv()
-    cot_side.start()
+    cot_side[0].start()
 
     def forward_group(inside, g, carry):
         def get(b):
@@ -276,6 +284,7 @@
     each(later, lambda e: states(end_f, planes_f, "fwd", e, True).start())
     lax.fori_loop(0, groups, functools.partial(forward_group, True), 0)
     w_step(1)
+    cot_side[1].start()
     for c in gat_copies:
         c.wait_recv()
     each(earlier, lambda e: states_got(end_f, planes_f, "fwd", e).wait_recv())
@@ -289,58 +298,70 @@
         state = incoming(planes_f, col_ref, g, outer, here, span, False)
         finish(state, put, rest_ref, row_ref, col_ref, inner, ends, g, blocks, False)
 
-    cot_side.wait_recv()
-    cot_next.start()
+    cot_side[0].wait_recv()
+    cot_next[0].start()
     for k in range(2, outer - 1):
         w_step(k)
     cot_core.wait_recv()
-    cot_next.wait_recv()
-
-
-    def right_copy(e):
-        return rdma(sum_send.at[e], sum_got.at[e + 1], "sum_right", e, outer, here + 1, mine)
-
-    def left_copy(e):
-        return rdma(sum_send.at[e], sum_got.at[e], "sum_left", e, outer, here - 1, mine)
-
-    def start_right(e):
-        sum_send[e] = dwp[e].astype(BF16)
-        right_copy(e).start()
-
-    def start_left(e):
-        sum_send[e] = dwp[e].astype(BF16)
-        left_copy(e).start()
-
-    def pass_right(e):
-        right_copy(e).wait_recv()
-        sum_send[e] = (dwp[e] + sum_got[e + 1].astype(F32)).astype(BF16)
-        right_copy(e).start()
-
-    def pass_left(e):
-        left_copy(e).wait_recv()
-        sum_send[e] = (dwp[e] + sum_got[e].astype(F32)).astype(BF16)
-        left_copy(e).start()
-
-    def weight_terms(order, end, start):
+    cot_next[0].wait_recv()
+
+
+    def right_copy(e, h):
+        return rdma(sum_send.at[e, :, halves[h]], sum_got.at[e + 1, :, halves[h]],
+                    "sum_right", e * 2 + h, 2 * outer, here + 1, mine)
+
+    def left_copy(e, h):
+        return rdma(sum_send.at[e, :, halves[h]], sum_got.at[e, :, halves[h]],
+                    "sum_left", e * 2 + h, 2 * outer, here - 1, mine)
+
+    def start_right(e, h):
+        c = halves[h]
+        sum_send[e, :, c] = dwp[e, :, c].astype(BF16)
+        right_copy(e, h).start()
+
+    def start_left(e, h):
+        c = halves[h]
+        sum_send[e, :, c] = dwp[e, :, c].astype(BF16)
+        left_copy(e, h).start()
+
+    def pass_right(e, h):
+        c = halves[h]
+        right_copy(e, h).wait_recv()
+        sum_send[e, :, c] = (dwp[e, :, c] + sum_got[e + 1, :, c].astype(F32)).astype(BF16)
+        right_copy(e, h).start()
+
+    def pass_left(e, h):
+        c = halves[h]
+        left_copy(e, h).wait_recv()
+        sum_send[e, :, c] = (dwp[e, :, c] + sum_got[e, :, c].astype(F32)).astype(BF16)
+        left_copy(e, h).start()
+
+    def weight_terms(order, end, start, h):
         for g in order:
-            dwp[g] = lax.dot_general(
-                mixed[:, g * lanes : (g + 1) * lanes], cots[...].reshape(span, width),
+            dwp[g, :, halves[h]] = lax.dot_general(
+                mixed[:, g * lanes : (g + 1) * lanes],
+                cots[:, :, halves[h]].reshape(span, half),
                 (((0,), (0,)), ((), ())), preferred_element_type=F32,
             )
             if g != end:
-                pl.when(here == end)(functools.partial(start, g))
+                pl.when(here == end)(functools.partial(start, g, h))
 
     lower = here < outer // 2
     upper = here >= outer // 2
-    pl.when(lower)(lambda: weight_terms(range(outer)[::-1], 0, start_right))
-    pl.when(upper)(lambda: weight_terms(range(outer), outer - 1, start_left))
-
-    def sum_step(k, near):
+    for h in range(2):
+        if h:
+            cot_side[h].wait_recv()
+            cot_next[h].start()
+            cot_next[h].wait_recv()
+        pl.when(lower)(lambda: weight_terms(range(outer)[::-1], 0, start_right, h))
+        pl.when(upper)(lambda: weight_terms(range(outer), outer - 1, start_left, h))
+
+    def sum_step(k, near, h):
         e, f = outer - k, k - 1
         right = jnp.logical_and(not_first, here < e)
         left = jnp.logical_and(not_last, here > f)
-        pl.when(jnp.logical_and(lower if near else upper, right))(functools.partial(pass_right, e))
-        pl.when(jnp.logical_and(upper if near else lower, left))(functools.partial(pass_left, f))
+        pl.when(jnp.logical_and(lower if near else upper, right))(functools.partial(pass_right, e, h))
+        pl.when(jnp.logical_and(upper if near else lower, left))(functools.partial(pass_left, f, h))
 
     for c in val_copies + gat_copies:
         c.wait_send()
@@ -377,7 +398,7 @@
         pl.when(k == outer - 1)(lambda: w_step(outer - 1))
         pl.when(here - k >= 0)(lambda: backward_group(here - k))
         pl.when(here + k < outer)(lambda: backward_group(here + k))
-        pl.when(k == 1)(lambda: sum_step(1, True))
+        pl.when(k == 1)(lambda: [sum_step(i, True, 0) for i in range(1, outer)] and None)
         return carry
 
     lax.fori_loop(1, outer, around, 0)
@@ -408,8 +429,8 @@
     out_far.start()
     out_send[1] = outp[core].astype(BF16)
     out_core.start()
-    for k in range(2, outer):
-        sum_step(k, True)
+    for k in range(1, outer):
+        sum_step(k, True, 1)
     out_far.wait_recv()
     out_send[2] = (outp[side] + out_got[0].astype(F32)).astype(BF16)
     out_side.start()
@@ -424,8 +445,9 @@
         finish(state, put, rest_ref, row_ref, col_ref, inner, ends, g, blocks, True)
     for c in vg_copies:
         c.start()
-    for k in range(1, outer):
-        sum_step(k, False)
+    for h in range(2):
+        for k in range(1, outer):
+            sum_step(k, False, h)
 
     def collect(buf, got, copies, dst):
         got[pl.ds(mine, 1)] = buf[pl.ds(mine, 1)]
@@ -447,11 +469,13 @@
     wgrad_ref[...] = dwp[here]
 
     def last_right():
-        right_copy(here).wait_recv()
+        for h in range(2):
+            right_copy(here, h).wait_recv()
         wgrad_ref[...] += sum_got[here + 1].astype(F32)
 
     def last_left():
-        left_copy(here).wait_recv()
+        for h in range(2):
+            left_copy(here, h).wait_recv()
         wgrad_ref[...] += sum_got[here].astype(F32)
 
     pl.when(not_first)(last_right)
@@ -459,7 +483,7 @@
 
     for c in gg_copies + vg_copies:
         c.wait_send()
-    for c in (cot_core, cot_side, cot_next, out_far, out_core, out_side):
+    for c in (cot_core, *cot_side, *cot_next, out_far, out_core, out_side):
         c.wait_send()
     each(later, lambda e: states(end_f, planes_f, "fwd", e, True).wait_send())
     each(earlier, lambda e: states(end_b, planes_b, "bwd", e, False).wait_send())
@@ -470,8 +494,8 @@
         pl.when(jnp.logical_and(not_first, here <= e))(
             lambda e=e: w_left(e, wbuf.at[e]).wait_send()
         )
-        pl.when(here < e)(lambda e=e: right_copy(e).wait_send())
-        pl.when(here > e)(lambda e=e: left_copy(e).wait_send())
+        pl.when(here < e)(lambda e=e: [right_copy(e, h).wait_send() for h in range(2)] and None)
+        pl.when(here > e)(lambda e=e: [left_copy(e, h).wait_send() for h in range(2)] and None)
     assert sum(s for _, s in spots.values()) <= send_sems.shape[0]
 
 
@@ -498,7 +522,7 @@
         ((INNER, tokens, width), F32), ((3, tokens, width), BF16), ((3, tokens, width), BF16),
         (slots, F32), ((outer + 1, rows, width), BF16), (slots, BF16),
     ]
-    sems = pltpu.SemaphoreType.DMA((18 + 9 * outer,))
+    sems = pltpu.SemaphoreType.DMA((20 + 11 * outer,))
     table = residue.T if lanes % 128 == 0 else residue
     args = (values, gating, out_weight, cotangent, table, decay_rate, skip_gain.reshape(ctx, lanes))
     out = jax.ShapeDtypeStruct((tokens, width), BF16)
@@ -516,24 +540,23 @@
             flops=2 * macs, bytes_accessed=6 * 2**20, transcendentals=0
         ),
     )(*args)
-    whole = [pl.BlockSpec(memory_space=pltpu.HBM)] * 4
+    steps = 2
+    blocks = [
+        pl.BlockSpec((r.shape[0] // steps, r.shape[1]), lambda i: (i, 0)) for r in results
+    ]
     return pl.pallas_call(
         hand_over,
+        grid=(steps,),
         out_shape=[jax.ShapeDtypeStruct(r.shape, r.dtype) for r in results],
-        in_specs=whole,
-        out_specs=whole,
-        scratch_shapes=[pltpu.SemaphoreType.DMA((4,))],
+        in_specs=blocks,
+        out_specs=blocks,
+        compiler_params=pltpu.CompilerParams(vmem_limit_bytes=58 * 2**20),
     )(*results)
 
 
 def hand_over(*refs):
-    copies = [
-        pltpu.make_async_copy(refs[i], refs[4 + i], refs[8].at[i]) for i in range(4)
-    ]
-    for c in copies:
-        c.start()
-    for c in copies:
-        c.wait()
+    for i in range(4):
+        refs[4 + i][...] = refs[i][...]
 
 
 def solution(mesh):

time: 173 us -> 95.8 us (0.55)
  Pallas kernels: 173 us -> 94.9 us
    pallas_call x1, Pallas kernels: 80.5 us -> 2.87 us  [per_device(): pl.pallas_call(hand_over, grid=(steps,), out_shape=[jax.ShapeDtypeStruct(...]
where the time goes in v5:
time: 95.8 us; the launch traced here: 95.6 us
  Pallas kernels  94.9 us (99%)
    pallas_call x1, Pallas kernels, per_device(): pl.pallas_call(functools.partial(kernel, outer), out_shape=[out, out, out...  92.1 us
    pallas_call x1, Pallas kernels, per_device(): pl.pallas_call(hand_over, grid=(steps,), out_shape=[jax.ShapeDtypeStruct(...  2.87 us

profile of v5, /device:TPU:0, one launch (start us, length us, event | category | flops | bytes accessed | tf_op | source)
XLA Modules:
  0.0 95.6 jit_solution(1098812419174369742)
XLA Ops:
  0.6 92.1 %shard_map.102 = (bf16[128,2048]{1,0:T(8,128)(2,1)}, bf16[128,2048]{1,0:T(8,128)(2,1)}, bf16[128,2048]{1,0:T(8,128)(2,1)}, f32[128,2048]{1,0:T(8,128)}) custom-call(bf16[128,2048]{1,0:T(8,128)(2,1)} %val_ref.1, bf16[128,2048]{1,0:T(8,128)(2,1)} %gat_ref.1, bf16[128,2048]{1,0:T(8,128)(2,1)} %w_ref.1, bf16[128,2048]{1,0:T(8,128)(2,1)} %cot_ref.1, ...), custom_call_target="tpu_custom_call" | custom-call | flops 3221225472 | bytes 6291456 | tf_op jit(solution)/shard_map/pallas_call | solution.py:530
  92.7 2.9 %shard_map.103 = (bf16[128,2048]{1,0:T(8,128)(2,1)}, bf16[128,2048]{1,0:T(8,128)(2,1)}, bf16[128,2048]{1,0:T(8,128)(2,1)}, f32[128,2048]{1,0:T(8,128)}) custom-call(bf16[128,2048]{1,0:T(8,128)(2,1)} %get-tuple-element.8.refs_0_, bf16[128,2048]{1,0:T(8,128)(2,1)} %get-tuple-element.9.refs_1_, bf16[128,2048]{1,0:T(8,128)(2,1)} %get-tuple-element.10.refs_2_, ...), custom_call_target="tpu_custom_call" | custom-call | tf_op jit(solution)/shard_map/pallas_call | solution.py:547
